TPU v7x, 32 devices: a whole 2x2x4 slice. The times are simulated.
32 devices in a mesh: grp: 4 (over y, core), band: 8 (over z, x).
Axes of the slice: x: 2, y: 2, z: 4, core: 2. Of those that a mesh axis runs over, the one named last changes fastest.
Arguments:
- prior_samples: bfloat16 [32, 69, 16, 1024], P('grp', None, 'band'), may hold values from -6 to 6
- conv1_weight: bfloat16 [3, 3, 256, 69], replicated, may hold values from -0.25 to 0.25
- conv1_bias: float32 [256], replicated, may hold values from -3 to 3
- conv2_weight: bfloat16 [3, 3, 69, 256], replicated, may hold values from -0.125 to 0.125
- conv2_bias: float32 [69], replicated, may hold values from -3 to 3
- obs_index: int32 [64, 256], P(('grp', 'band')), may hold values from 0 to 17663
- obs_values: float32 [64, 256], P(('grp', 'band')), may hold values from -6 to 6
- obs_prec: float32 [64, 256], P(('grp', 'band')), may hold values from 0.25 to 4
- neighbours: int32 [64, 8], P(('grp', 'band')), may hold values from 0 to 63
- loc_weight: float32 [64, 8], P(('grp', 'band')), may hold values from 0.2 to 1
Outputs:
- analysis: float32 [32, 69, 16, 1024], P(None, None, 'band', 'grp')
Inputs may be any that keep to these rules, and one draw needn't show every extreme that they name: `neighbours`: neighbour patch numbers; a number may repeat or name the patch itself. `obs_index`: observed entry as channel * 256 + column within the patch.
All inputs are finite; a program needn't handle non-finite values.
Results may differ from a plain program's by a relative error of at most 0.0021.
Values may be sent and summed in bfloat16 or wider, within the bound.
A program may use at most 128 MiB of HBM per device.

v0:
```python
import jax
import jax.numpy as jnp
from jax import lax
from jax.sharding import PartitionSpec as P

NS_ITERS = 6


def padded_2(cells, sides, width):
    for axis, dim in sides:
        count = lax.axis_size(axis)
        ends = count - 1
        head = lax.slice_in_dim(cells, 0, width, axis=dim)
        tail = lax.slice_in_dim(cells, cells.shape[dim] - width, cells.shape[dim], axis=dim)
        cells = jnp.concatenate(
            [
                lax.ppermute(tail, axis, [(i, (i + 1) % count) for i in range(ends)]),
                cells,
                lax.ppermute(head, axis, [((i + 1) % count, i) for i in range(ends)]),
            ],
            axis=dim,
        )
    return cells


def from_behind(block, axis, distance):
    devices = range(lax.axis_size(axis))
    route = [(i - distance, i) for i in devices if i - distance in devices]
    return lax.ppermute(block, axis, route)


def convolve(padded, kernel, height):
    summed = jnp.zeros((kernel.shape[2], height, padded.shape[2]), jnp.float32)
    for row_shift in range(3):
        window = padded[:, row_shift : row_shift + height, :]
        for col_shift in range(3):
            shifted = jnp.roll(window, 1 - col_shift, axis=2)
            summed = summed + jnp.einsum(
                "oc,crl->orl",
                kernel[row_shift, col_shift],
                shifted,
                preferred_element_type=jnp.float32,
            )
    return summed


def grams_of(perturb, obs_prec, innovation):
    highest = lax.Precision.HIGHEST
    gram_local = jnp.einsum("pmo,po,pno->pmn", perturb, obs_prec, perturb, precision=highest)
    pull_vec = jnp.einsum("pmo,po->pm", perturb, obs_prec * innovation, precision=highest)
    return (gram_local, pull_vec)


def on_device(
    prior_samples,
    conv1_weight,
    conv1_bias,
    conv2_weight,
    conv2_bias,
    obs_index,
    obs_values,
    obs_prec,
    neighbours,
    loc_weight,
):
    highest = lax.Precision.HIGHEST
    height = prior_samples.shape[2]
    padded = padded_2(prior_samples, (("band", 2),), 1)

    def first_layer(member):
        return jax.nn.silu(
            convolve(member, conv1_weight, height) + conv1_bias[:, None, None]
        ).astype(jnp.bfloat16)

    hidden_fields = lax.map(first_layer, padded)
    northern_halo = from_behind(hidden_fields[:, :, height - 1 :, :], "band", 1)
    southern_halo = from_behind(hidden_fields[:, :, :1, :], "band", -1)

    def output_layer(inputs):
        member, own_rows, above_row, below_row = inputs
        extended = jnp.concatenate([above_row, own_rows, below_row], axis=1)
        summed = (
            member.astype(jnp.float32)
            + convolve(extended, conv2_weight, height)
            + conv2_bias[:, None, None]
        )
        return summed.astype(jnp.bfloat16)

    predicted_samples = lax.map(
        output_layer, (prior_samples, hidden_fields, northern_halo, southern_halo)
    )
    patch_block_slice = lax.all_to_all(
        predicted_samples, "grp", split_axis=3, concat_axis=0, tiled=True
    )
    ensemble = patch_block_slice.shape[0]
    channels = patch_block_slice.shape[1]
    patch_width = patch_block_slice.shape[3]
    realization_grid = jnp.transpose(patch_block_slice, (2, 0, 1, 3)).reshape(
        height, ensemble, channels * patch_width
    )
    count_obs = obs_index.shape[1]
    chosen = jnp.broadcast_to(obs_index[:, None, :], (height, ensemble, count_obs))
    predicted = jnp.take_along_axis(realization_grid, chosen, axis=2).astype(jnp.float32)
    predicted_mean = jnp.mean(predicted, axis=1)
    perturb = predicted - predicted_mean[:, None, :]
    innovation = obs_values - predicted_mean
    gram_local, pull_vec = grams_of(perturb, obs_prec, innovation)
    total_patches = height * lax.axis_size("grp") * lax.axis_size("band")
    patch_ids = jnp.arange(total_patches, dtype=jnp.int32)
    matches = (neighbours[:, :, None] == patch_ids[None, None, :]).astype(jnp.float32)
    spread_weights = jnp.sum(loc_weight[:, :, None] * matches, axis=1)
    piece_gram, piece_pull = grams_of(
        lax.all_gather(perturb, ("grp", "band"), axis=0, tiled=True),
        lax.all_gather(obs_prec, ("grp", "band"), axis=0, tiled=True),
        lax.all_gather(innovation, ("grp", "band"), axis=0, tiled=True),
    )
    gram_sum = jnp.einsum("pj,jab->pab", spread_weights, piece_gram, precision=highest)
    pull_sum = jnp.einsum("pj,ja->pa", spread_weights, piece_pull, precision=highest)
    identity = jnp.broadcast_to(jnp.eye(ensemble, dtype=jnp.float32), (height, ensemble, ensemble))
    matrix = (ensemble - 1.0) * identity + gram_local + gram_sum
    pulled = pull_vec + pull_sum
    norm_scale = jnp.sqrt(jnp.sum(matrix * matrix, axis=(1, 2)))
    sqrt_iter = matrix / norm_scale[:, None, None]
    inverse_root = identity
    for sweep in range(NS_ITERS):
        half_step = 1.5 * identity - 0.5 * jnp.einsum(
            "pab,pbc->pac", inverse_root, sqrt_iter, precision=highest
        )
        sqrt_iter = jnp.einsum("pab,pbc->pac", sqrt_iter, half_step, precision=highest)
        inverse_root = jnp.einsum("pab,pbc->pac", half_step, inverse_root, precision=highest)
    once_applied = jnp.einsum("pab,pb->pa", inverse_root, pulled, precision=highest)
    mean_weight = (
        jnp.einsum("pab,pb->pa", inverse_root, once_applied, precision=highest)
        / norm_scale[:, None]
    )
    transform = (jnp.sqrt(ensemble - 1.0) / jnp.sqrt(norm_scale))[
        :, None, None
    ] * inverse_root + mean_weight[:, :, None]
    field = realization_grid.astype(jnp.float32)
    centre = jnp.mean(field, axis=1)
    spread = field - centre[:, None, :]
    analysed = centre[:, None, :] + jnp.einsum("pkm,pkc->pmc", transform, spread, precision=highest)
    return analysed.reshape(height, ensemble, channels, patch_width).transpose(1, 2, 0, 3)


def solution(mesh):
    placed = (
        P("grp", None, "band", None),
        P(),
        P(),
        P(),
        P(),
        P(("grp", "band"), None),
        P(("grp", "band"), None),
        P(("grp", "band"), None),
        P(("grp", "band"), None),
        P(("grp", "band"), None),
    )
    return jax.shard_map(
        on_device,
        mesh=mesh,
        in_specs=placed,
        out_specs=P(None, None, "band", "grp"),
        check_vma=False,
    )
```

profile of v0, /device:TPU:0, one launch (start us, length us, event | category | flops | bytes accessed | tf_op | source)
XLA Modules:
  0.0 815.5 jit_solution(15843688652743729444)
XLA Ops:
  6.5 5.9 fusion.156
  12.9 6.0 collective-permute-start
  18.9 1.4 copy.95
  22.4 43.9 %collective-permute-done = bf16[8,69,1,1024]{3,0,2,1:T(8,128)(2,1)} collective-permute-done((bf16[8,69,1,1024]{3,0,2,1:T(8,128)(2,1)S(1)}, bf16[8,69,1,1024]{3,0,2,1:T(8,128)(2,1)}, u32[]{:S(2)}, u32[]{:S(2)}) %collective-permute-start) | collective-permute-done | bytes 1130528 | tf_op jit(solution)/shard_map/ppermute | solution.py:17
  66.2 1.9 copy.66
  68.1 1.9 copy.68
  70.1 2.5 pad_maximum_fusion.6
  72.6 73.3 %while.20 = (s32[]{:T(128)}, bf16[8,256,2,1024]{3,1,2,0:T(8,128)(2,1)}, bf16[8,69,4,1024]{3,1,2,0:T(8,128)(2,1)}, bf16[3,3,256,69]{2,3,1,0:T(8,128)(2,1)S(1)}, f32[256]{0:T(256)S(1)}, /*index=5*/s32[]{:T(128)}) while((s32[]{:T(128)}, bf16[8,256,2,1024]{3,1,2,0:T(8,128)(2,1)}, bf16[8,69,4,1024]{3,1,2,0:T(8,128)(2,1)}, ...), condition=%wide.region_1.2_spmd, body=%wide.region_0.1_spmd.sunk | while | flops 661897216 | bytes 47412808 | solution.py:75
  145.9 6.1 fusion.155
  151.9 6.5 collective-permute-start.2
  158.4 1.5 collective-permute-start.3
  159.9 175.7 %collective-permute-done.2 = bf16[8,256,1,1024]{3,1,2,0:T(8,128)(2,1)} collective-permute-done((bf16[8,256,1,1024]{3,1,2,0:T(8,128)(2,1)}, bf16[8,256,1,1024]{3,1,2,0:T(8,128)(2,1)}, u32[]{:S(2)}, u32[]{:S(2)}) %collective-permute-start.2) | collective-permute-done | bytes 4194336 | tf_op jit(solution)/shard_map/ppermute | solution.py:29
  335.6 70.6 %while.21 = (s32[]{:T(128)}, bf16[8,69,2,1024]{3,1,2,0:T(8,128)(2,1)S(1)}, bf16[8,69,2,1024]{3,1,2,0:T(8,128)(2,1)}, bf16[8,256,1,1024]{3,1,2,0:T(8,128)(2,1)}, ...) while((s32[]{:T(128)}, ...), condition=%wide.region_3.4_spmd, body=%wide.region_2.3_spmd.sunk | while | flops 675929088 | bytes 41343592 | solution.py:89
  338.2 1.4 fusion.307
  347.0 1.4 fusion.307
  364.6 1.4 fusion.307
  373.5 1.4 fusion.307
  406.2 7.7 copy.73
  413.8 5.0 all-to-all-start
  419.0 48.1 %all-to-all-done = bf16[8,69,2,1024]{1,2,0,3:T(2,128)(2,1)} async-done(((bf16[8,69,2,1024]{1,2,0,3:T(2,128)(2,1)}), bf16[8,69,2,1024]{1,2,0,3:T(2,128)(2,1)}, u32[]{:S(2)}, u32[]{:S(2)}) %all-to-all-start) | async-done | bytes 2261024 | tf_op jit(solution)/shard_map/all_to_all | solution.py:92
  467.1 10.5 %copy.90 = bf16[8,69,2,4,256]{4,3,0,2,1:T(4,128)(2,1)S(1)} copy(bf16[8,69,2,4,256]{1,2,0,4,3:T(2,128)(2,1)} %bitcast.45) | data formatting | bytes 4521984 | tf_op jit(solution)/shard_map/all_to_all | solution.py:92
  477.6 2.7 copy.91
  480.3 3.1 reshape.45
  483.4 159.3 %gather_fusion = bf16[16384]{0:T(1024)(128)(2,1)S(1)} fusion(bf16[2,32,17664]{2,1,0:T(8,128)(2,1)S(1)} %reshape.45, s32[16384]{0:T(1024)S(1)} %bitcast.273), kind=kCustom, calls=%fused_computation | custom fusion | bytes 262144 | tf_op jit(solution)/shard_map/jit(take_along_axis)/gather | solution.py:103
  643.4 67.6 %all-gather = f32[32,2,256]{2,1,0:T(2,128)S(1)} all-gather(f32[1,2,256]{2,1,0:T(2,128)S(1)} %bitcast.281), channel_id=1, replica_groups=mesh['grp'=4,'band'=8] {'grp','band'}, dimensions={0}, use_global_device_ids=true | all-gather | bytes 67584 | tf_op jit(solution)/shard_map/all_gather | solution.py:114
  711.3 63.9 %all-gather.1 = f32[32,2,256]{2,1,0:T(2,128)S(1)} all-gather(f32[1,2,256]{2,1,0:T(2,128)S(1)} %get-tuple-element.172), channel_id=1, replica_groups=mesh['grp'=4,'band'=8] {'grp','band'}, dimensions={0}, use_global_device_ids=true | all-gather | bytes 67584 | tf_op jit(solution)/shard_map/all_gather | solution.py:115
  775.4 2.9 convert_reduce_fusion
  778.4 4.3 fusion.118
  787.2 1.9 fusion.132
  789.7 5.8 convolution_add_fusion.7
  795.5 5.2 reshape.46
  800.7 7.9 copy.80
  (289 shorter events, 146.1 us)
Async XLA Ops:
  12.9 8.7 %copy-start = (bf16[8,69,2,1024]{3,2,1,0:T(2,128)(2,1)S(1)}, bf16[8,69,2,1024]{3,2,1,0:T(2,128)(2,1)}, u32[]{:S(2)}) copy-start(bf16[8,69,2,1024]{3,2,1,0:T(2,128)(2,1)} %param.14) | copy-start | bytes 6782980
  12.9 53.4 %collective-permute-start = (bf16[8,69,1,1024]{3,0,2,1:T(8,128)(2,1)S(1)}, bf16[8,69,1,1024]{3,0,2,1:T(8,128)(2,1)}, u32[]{:S(2)}, u32[]{:S(2)}) collective-permute-start(bf16[8,69,1,1024]{3,0,2,1:T(8,128)(2,1)S(1)} %copy.94), channel_id=1, source_target_pairs={{0,1},{1,2},{2,3},{3,4},{4,5},{5,6},{6,7},{8,9},{9,10},{10,11},{11... | collective-permute-start | bytes 3391496 | tf_op jit(solution)/shard_map/ppermute | solution.py:17
  20.3 47.8 %collective-permute-start.1 = (bf16[8,69,1,1024]{3,0,2,1:T(8,128)(2,1)}, bf16[8,69,1,1024]{3,0,2,1:T(8,128)(2,1)}, u32[]{:S(2)}, u32[]{:S(2)}) collective-permute-start(bf16[8,69,1,1024]{3,0,2,1:T(8,128)(2,1)} %copy.95), channel_id=1, source_target_pairs={{1,0},{2,1},{3,2},{4,3},{5,4},{6,5},{7,6},{9,8},{10,9},{11,10},{12... | collective-permute-start | bytes 3391496 | tf_op jit(solution)/shard_map/ppermute | solution.py:19
  22.3 47.7 %copy-start.3 = (bf16[8,69,2,1024]{3,1,2,0:T(8,128)(2,1)}, bf16[8,69,2,1024]{3,1,2,0:T(8,128)(2,1)S(1)}, u32[]{:S(2)}) copy-start(bf16[8,69,2,1024]{3,1,2,0:T(8,128)(2,1)S(1)} %copy.71) | copy-start | bytes 6782980
  70.0 2.5 copy-start.4
  70.0 2.5 copy-start.7
  145.9 189.7 %copy-start.5 = (bf16[3,3,69,256]{3,2,1,0:T(8,128)(2,1)S(1)}, bf16[3,3,69,256]{3,2,1,0:T(8,128)(2,1)}, u32[]{:S(2)}) copy-start(bf16[3,3,69,256]{3,2,1,0:T(8,128)(2,1)} %param.17) | copy-start | bytes 953860
  145.9 189.7 %copy-start.12 = (f32[69]{0:T(128)S(1)}, f32[69]{0:T(128)}, u32[]{:S(2)}) copy-start(f32[69]{0:T(128)} %param.18) | copy-start | bytes 832
  151.9 183.6 %collective-permute-start.2 = (bf16[8,256,1,1024]{3,1,2,0:T(8,128)(2,1)}, bf16[8,256,1,1024]{3,1,2,0:T(8,128)(2,1)}, u32[]{:S(2)}, u32[]{:S(2)}) collective-permute-start(bf16[8,256,1,1024]{3,1,2,0:T(8,128)(2,1)} %get-tuple-element.169), channel_id=1, source_target_pairs={{0,1},{1,2},{2,3},{3,4},{4,5},{5,6},{6,7},{8,9},{9,10},{10,11},{11... | collective-permute-start | bytes 12582920 | tf_op jit(solution)/shard_map/ppermute | solution.py:29
  158.4 177.2 %collective-permute-start.3 = (bf16[8,256,1,1024]{3,1,2,0:T(8,128)(2,1)}, bf16[8,256,1,1024]{3,1,2,0:T(8,128)(2,1)}, u32[]{:S(2)}, u32[]{:S(2)}) collective-permute-start(bf16[8,256,1,1024]{3,1,2,0:T(8,128)(2,1)} %get-tuple-element.168), channel_id=1, source_target_pairs={{1,0},{2,1},{3,2},{4,3},{5,4},{6,5},{7,6},{9,8},{10,9},{11,10},{12... | collective-permute-start | bytes 12582920 | tf_op jit(solution)/shard_map/ppermute | solution.py:29
  413.8 5.1 copy-start.6
  413.8 53.2 %all-to-all-start = ((bf16[8,69,2,1024]{1,2,0,3:T(2,128)(2,1)}), bf16[8,69,2,1024]{1,2,0,3:T(2,128)(2,1)}, u32[]{:S(2)}, u32[]{:S(2)}) async-start(bf16[8,69,2,1024]{1,2,0,3:T(2,128)(2,1)} %copy.73), calls=%async_computation | async-start | bytes 8388608 | tf_op jit(solution)/shard_map/all_to_all | solution.py:92
  418.9 359.5 %all-gather.4.cloned.1.call-start = ((), (), s32[]{:S(2)}) async-start(), calls=%async_computation.1 | async-start | bytes 2162688 | tf_op jit(solution)/shard_map/all_gather | solution.py:113
  477.6 2.7 copy-start.1
  483.4 159.4 %copy-start.8 = (f32[2,256]{1,0:T(2,128)S(1)}, f32[2,256]{1,0:T(2,128)}, u32[]{:S(2)}) copy-start(f32[2,256]{1,0:T(2,128)} %param.21) | copy-start | bytes 6148
  483.4 159.4 %copy-start.9 = (f32[2,256]{1,0:T(2,128)S(1)}, f32[2,256]{1,0:T(2,128)}, u32[]{:S(2)}) copy-start(f32[2,256]{1,0:T(2,128)} %param.20) | copy-start | bytes 6148
  483.4 227.8 %copy-start.10 = (f32[2,8]{1,0:T(2,128)S(1)}, f32[2,8]{1,0:T(2,128)}, u32[]{:S(2)}) copy-start(f32[2,8]{1,0:T(2,128)} %param.23) | copy-start | bytes 196
  483.4 227.8 %copy-start.11 = (s32[2,8]{1,0:T(2,128)S(1)}, s32[2,8]{1,0:T(2,128)}, u32[]{:S(2)}) copy-start(s32[2,8]{1,0:T(2,128)} %param.22) | copy-start | bytes 196
  782.7 4.5 copy-start.2
Sparse Core Ops, SparseCore 0:
  643.6 57.9 all-gather.3
where the time goes:
time: 817 us; the launch traced here: 815 us
  waiting for transfers between devices  268 us (33%)
  local copies, waits for them, and re-layouts  261 us (32%)
  blocking collectives  131 us (16%)
  matrix products  102 us (12%)
  starting transfers between devices  20.3 us (2%)
  other arithmetic  18.5 us (2%)
  between operations  13.9 us (2%)
    ppermute x2, waiting for transfers between devices, from_behind(): return lax.ppermute(block, axis, route)  176 us
    gather x2, local copies, waits for them, and re-layouts, on_device(): jnp.take_along_axis(realization_grid, chosen, axis=2).astype(jnp.float32)  159 us
    dot_general x144, matrix products, convolve(): jnp.einsum('oc,crl->orl', kernel[row_shift, col_shift], shifted, preferre...  84.6 us
    all_gather x1, blocking collectives, on_device(): lax.all_gather(obs_prec, ('grp', 'band'), axis=0, tiled=True)  67.6 us
    all_gather x1, blocking collectives, on_device(): lax.all_gather(innovation, ('grp', 'band'), axis=0, tiled=True)  63.9 us
    all_to_all x1, waiting for transfers between devices, on_device(): lax.all_to_all(predicted_samples, 'grp', split_axis=3, concat_axis=0, til...  48.1 us
    ppermute x1, waiting for transfers between devices, padded_2(): lax.ppermute(tail, axis, [(i, (i + 1) % count) for i in range(ends)])  43.9 us
    squeeze x16, local copies, waits for them, and re-layouts, on_device(): lax.map(output_layer, (prior_samples, hidden_fields, northern_halo, south...  20.6 us
  transfers between devices with their start and end apart: 6, of which 3 were waited for; matrix products, arithmetic and copies ran while one was open for 1% of the time, Pallas kernels for 0%

commit v1 on v0

v1 whole, which is shorter than its diff:
```python
import functools

import jax
import jax.numpy as jnp
from jax import lax
from jax.experimental import pallas as pl
from jax.experimental.pallas import tpu as pltpu
from jax.sharding import PartitionSpec as P

NS_ITERS = 6
PAIR = 2
ROWK = 224
SMEM = pl.BlockSpec(memory_space=pltpu.SMEM)
VMEM = pl.BlockSpec(memory_space=pltpu.VMEM)
HIGH = lax.Precision.HIGHEST


def forecast_kernel(info, own, near, far, w1, b1, w2, b2, *rest, chans, hid, lon, groups):
    outs, (ext, hidden, fore) = rest[:groups], rest[groups:]
    odd, grp = info[0], info[1]
    width = lon // groups

    for member in range(PAIR):
        for source, base in ((own, 2), (near, 4 * (1 - odd)), (far, 4 * odd)):
            for row in range(2):
                x = source[member, row].astype(jnp.float32)
                shifted = [
                    pltpu.roll(x, 1, 1),
                    x,
                    pltpu.roll(x, lon - 1, 1),
                    jnp.zeros((ROWK - 3 * chans, lon), jnp.float32),
                ]
                ext[base + row] = jnp.concatenate(shifted, axis=0).astype(jnp.bfloat16)

        for row in range(4):
            if row == 0:
                keep = info[2]
            elif row == 3:
                keep = info[3]
            else:
                keep = None

            def tile(n, carry, row=row, keep=keep):
                cols = pl.ds(pl.multiple_of(n * 256, 256), 256)
                window = ext[row : row + 3, :, cols].reshape(3 * ROWK, 256)
                h = jnp.dot(w1[...], window, preferred_element_type=jnp.float32) + b1[...]
                h = 0.5 * h
                h = h + h * jnp.tanh(h)
                if keep is not None:
                    h = jnp.where(keep > 0, h, 0.0)
                hidden[row * hid : (row + 1) * hid, cols] = h.astype(jnp.bfloat16)
                return carry

            lax.fori_loop(0, lon // 256, tile, 0, unroll=2)

        for row in range(2):
            summed = jnp.dot(
                w2[...],
                hidden[row * hid : (row + 3) * hid, :],
                preferred_element_type=jnp.float32,
            )
            out = (
                pltpu.roll(summed[:chans], 1, 1)
                + summed[chans : 2 * chans]
                + pltpu.roll(summed[2 * chans :], lon - 1, 1)
                + own[member, row].astype(jnp.float32)
                + b2[...]
            )
            for part in range(groups):
                piece = out[:, part * width : (part + 1) * width]
                fore[part, row, :, member * 8 : (member + 1) * 8, :] = piece.reshape(
                    chans // 8, 8, width
                )

    for step in range(groups):
        for row in range(2):
            block = fore[jnp.bitwise_xor(grp, step), row]
            outs[step][row] = block.reshape(chans * PAIR, width).astype(jnp.bfloat16)


def gram_kernel(info, *rest, pairs, groups, chans, members, nobs, width):
    slabs = rest[: groups * pairs]
    chan, col, obs, prec, field, packed, pred = rest[groups * pairs :]
    grp = info[1]
    blocks = chans // 8
    depth = chans * PAIR
    lane = lax.broadcasted_iota(jnp.int32, (nobs, depth), 1)
    lane_chan = (lane // 16) * 8 + lane % 8
    lane_member = (lane // 8) % 2
    col_iota = lax.broadcasted_iota(jnp.int32, (nobs, width), 1)
    ones = jnp.ones((8, width), jnp.bfloat16)
    packed[...] = jnp.zeros_like(packed)
    for row in range(2):
        pick_chan = lane_chan == chan[:, row : row + 1]
        selects = [
            jnp.where(pick_chan & (lane_member == v), 1.0, 0.0).astype(jnp.bfloat16)
            for v in range(PAIR)
        ]
        pick_col = col_iota == col[:, row : row + 1]
        for step in range(groups):
            source = jnp.bitwise_xor(grp, step)
            for pair in range(pairs):
                slab = slabs[pair * groups + step]
                first = source * (pairs * PAIR) + pair * PAIR
                values = slab[row]
                for block in range(blocks):
                    rows = pl.ds(pl.multiple_of(first * 8, 16), 16)
                    field[row, block, rows, :] = values[block * 16 : (block + 1) * 16, :]
                for v in range(PAIR):
                    g = jnp.dot(selects[v], values, preferred_element_type=jnp.float32)
                    g = jnp.where(pick_col, g, 0.0).astype(jnp.bfloat16)
                    line = lax.dot_general(
                        ones, g, (((1,), (1,)), ((), ())), preferred_element_type=jnp.float32
                    )
                    pred[first + v] = line
        predicted = pred[:, 0, :]
        mean = jnp.sum(predicted, axis=0, keepdims=True) * (1.0 / members)
        perturb = predicted - mean
        innovation = obs[row : row + 1, :] - mean
        both = jnp.concatenate([perturb, jnp.broadcast_to(innovation, (8, nobs))], axis=0)
        packed[:, row * 64 : row * 64 + members + 8] = lax.dot_general(
            perturb * prec[row : row + 1, :],
            both,
            (((1,), (1,)), ((), ())),
            precision=HIGH,
            preferred_element_type=jnp.float32,
        )


def analysis_kernel(neighbours, weights, mine, gathered, field, out, *, members, chans, real, width):
    eye = (
        lax.broadcasted_iota(jnp.int32, (members, members), 0)
        == lax.broadcasted_iota(jnp.int32, (members, members), 1)
    ).astype(jnp.float32)
    wide = members * 8
    expand = (
        lax.broadcasted_iota(jnp.int32, (wide, members), 0) // 8
        == lax.broadcasted_iota(jnp.int32, (wide, members), 1)
    ).astype(jnp.bfloat16)
    same = (
        lax.broadcasted_iota(jnp.int32, (wide, wide), 0) % 8
        == lax.broadcasted_iota(jnp.int32, (wide, wide), 1) % 8
    )

    def dot(a, b):
        return jnp.dot(a, b, precision=HIGH, preferred_element_type=jnp.float32)

    state = []
    for row in range(2):
        total = mine[...] if row == 0 else pltpu.roll(mine[...], 64, 1)
        for k in range(neighbours.shape[1]):
            j = neighbours[row, k]
            gram = gathered[j // 2]
            gram = jnp.where(j % 2 == 1, pltpu.roll(gram, 64, 1), gram)
            total = total + weights[row, k] * gram
        matrix = total[:, :members] + (members - 1.0) * eye
        norm = jnp.sqrt(jnp.sum(matrix * matrix, keepdims=True))
        state.append([matrix / norm, eye, total, norm])
    for sweep in range(NS_ITERS):
        halves = [1.5 * eye - 0.5 * dot(inv, root) for root, inv, _, _ in state]
        for entry, half in zip(state, halves):
            entry[0] = dot(entry[0], half)
            entry[1] = dot(half, entry[1])
    for row in range(2):
        _, inv, total, norm = state[row]
        mean_weight = dot(inv, dot(inv, total))[:, members : members + 1] / norm
        transform = (jnp.sqrt(members - 1.0) / jnp.sqrt(norm)) * inv + mean_weight
        transform = transform + (1.0 - jnp.sum(transform, axis=0, keepdims=True)) * (1.0 / members)
        spread = []
        for piece in range(3):
            part = transform.astype(jnp.bfloat16)
            transform = transform - part.astype(jnp.float32)
            tall = lax.dot_general(
                expand, part, (((1,), (1,)), ((), ())), preferred_element_type=jnp.float32
            ).astype(jnp.bfloat16)
            full = lax.dot_general(
                tall, expand, (((1,), (1,)), ((), ())), preferred_element_type=jnp.float32
            )
            spread.append(jnp.where(same, full, 0.0).astype(jnp.bfloat16))
        for block in range(chans // 8):
            x = field[row, block]
            y = jnp.dot(spread[0], x, preferred_element_type=jnp.float32)
            y = y + jnp.dot(spread[1], x, preferred_element_type=jnp.float32)
            y = y + jnp.dot(spread[2], x, preferred_element_type=jnp.float32)
            count = min(8, real - block * 8)
            for member in range(members):
                for half in range(width // 128):
                    start = (member * real + block * 8) * 4 + half * 2 + row
                    out[pl.ds(start, count, stride=4), :] = y[
                        member * 8 : member * 8 + count, half * 128 : (half + 1) * 128
                    ]


def on_device(
    prior_samples,
    conv1_weight,
    conv1_bias,
    conv2_weight,
    conv2_bias,
    obs_index,
    obs_values,
    obs_prec,
    neighbours,
    loc_weight,
):
    bands = lax.axis_size("band")
    groups = lax.axis_size("grp")
    own_members, real, height, lon = prior_samples.shape
    members = own_members * groups
    hid = conv1_weight.shape[2]
    width = lon // groups
    nobs = obs_index.shape[1]
    chans = -(-real // 8) * 8
    band = lax.axis_index("band")
    grp = lax.axis_index("grp")
    info = jnp.stack([band % 2, grp, band > 0, band < bands - 1]).astype(jnp.int32)

    w1 = jnp.pad(conv1_weight, ((0, 0), (0, 0), (0, 0), (0, chans - real)))
    w1 = jnp.transpose(w1, (2, 0, 1, 3)).reshape(hid, 3, 3 * chans)
    w1 = jnp.pad(w1, ((0, 0), (0, 0), (0, ROWK - 3 * chans))).reshape(hid, 3 * ROWK)
    w2 = jnp.pad(conv2_weight, ((0, 0), (0, 0), (0, chans - real), (0, 0)))
    w2 = jnp.transpose(w2, (1, 2, 0, 3)).reshape(3 * chans, 3 * hid)
    b1 = conv1_bias[:, None]
    b2 = jnp.pad(conv2_bias, (0, chans - real))[:, None]

    swap = [(i, i ^ 1) for i in range(bands)]
    forward = [(i, i - 2) for i in range(3, bands, 2)] + [(i, i + 2) for i in range(0, bands - 2, 2)]
    pairs = own_members // PAIR
    depth = chans * PAIR
    forecast = pl.pallas_call(
        functools.partial(forecast_kernel, chans=chans, hid=hid, lon=lon, groups=groups),
        out_shape=[jax.ShapeDtypeStruct((height, depth, width), jnp.bfloat16)] * groups,
        in_specs=[SMEM] + [VMEM] * 7,
        out_specs=[VMEM] * groups,
        scratch_shapes=[
            pltpu.VMEM((6, ROWK, lon), jnp.bfloat16),
            pltpu.VMEM((4 * hid, lon), jnp.bfloat16),
            pltpu.VMEM((groups, height, chans // 8, 8 * PAIR, width), jnp.float32),
        ],
        compiler_params=pltpu.CompilerParams(vmem_limit_bytes=40 * 2**20),
        cost_estimate=pl.CostEstimate(
            flops=2 * PAIR * 6 * hid * 768 * lon, bytes_accessed=4 * 2**20, transcendentals=0
        ),
        name="forecast",
    )
    slabs = []
    for pair in range(pairs):
        own = prior_samples[pair * PAIR : (pair + 1) * PAIR]
        own = jnp.pad(jnp.transpose(own, (0, 2, 1, 3)), ((0, 0), (0, 0), (0, chans - real), (0, 0)))
        near = lax.ppermute(own, "band", swap)
        far = lax.ppermute(near, "band", forward)
        pieces = forecast(info, own, near, far, w1, b1, w2, b2)
        for step in range(groups):
            piece = pieces[step]
            if step:
                piece = lax.ppermute(piece, "grp", [(i, i ^ step) for i in range(groups)])
            slabs.append(piece)

    chan = (obs_index // width).T
    col = (obs_index % width).T
    field, packed = pl.pallas_call(
        functools.partial(
            gram_kernel,
            pairs=pairs,
            groups=groups,
            chans=chans,
            members=members,
            nobs=nobs,
            width=width,
        ),
        out_shape=[
            jax.ShapeDtypeStruct((height, chans // 8, members * 8, width), jnp.bfloat16),
            jax.ShapeDtypeStruct((members, 128), jnp.float32),
        ],
        in_specs=[SMEM] + [VMEM] * (len(slabs) + 4),
        out_specs=[VMEM] * 2,
        scratch_shapes=[pltpu.VMEM((members, 8, nobs), jnp.float32)],
        compiler_params=pltpu.CompilerParams(vmem_limit_bytes=40 * 2**20),
        name="grams",
    )(info, *slabs, chan, col, obs_values, obs_prec)
    gathered = lax.all_gather(packed, ("grp", "band"), axis=0)
    out = pl.pallas_call(
        functools.partial(analysis_kernel, members=members, chans=chans, real=real, width=width),
        out_shape=jax.ShapeDtypeStruct((members * real * 2 * height, 128), jnp.float32),
        in_specs=[SMEM, SMEM, VMEM, VMEM, VMEM],
        out_specs=VMEM,
        compiler_params=pltpu.CompilerParams(vmem_limit_bytes=40 * 2**20),
        name="analyse",
    )(neighbours, loc_weight, packed, gathered, field)
    out = out.reshape(members, real, width // 128, height, 128)
    return jnp.transpose(out, (0, 1, 3, 2, 4)).reshape(members, real, height, width)


def solution(mesh):
    placed = (
        P("grp", None, "band", None),
        P(),
        P(),
        P(),
        P(),
        P(("grp", "band"), None),
        P(("grp", "band"), None),
        P(("grp", "band"), None),
        P(("grp", "band"), None),
        P(("grp", "band"), None),
    )
    return jax.shard_map(
        on_device,
        mesh=mesh,
        in_specs=placed,
        out_specs=P(None, None, "band", "grp"),
        check_vma=False,
    )
```

time: 817 us -> 213 us (0.26)
  local copies, waits for them, and re-layouts: 261 us -> 6.33 us
  waiting for transfers between devices: 268 us -> 42.3 us
  matrix products: 102 us -> 0 us
  Pallas kernels: 0 us -> 62.1 us
  blocking collectives: 131 us -> 70.8 us
  other arithmetic: 18.5 us -> 0.21 us
  between operations: 13.9 us -> 0.33 us
  starting transfers between devices: 20.3 us -> 31 us
    ppermute x4 -> x20, waiting for transfers between devices: 220 us -> 42.3 us  [the longest x4 31.7 us: on_device(): near = lax.ppermute(own, 'band', swap)]
    gather x2 -> x0, local copies, waits for them, and re-layouts: 159 us -> none  [on_device(): jnp.take_along_axis(realization_grid, chosen, axis=2).astype(jnp.float32)]
    dot_general x170 -> x0, matrix products: 102 us -> none  [the longest x144 84.6 us: convolve(): jnp.einsum('oc,crl->orl', kernel[row_shift, col_shift], shifted, preferre...]
    pallas_call x0 -> x6, Pallas kernels: none -> 62.1 us  [the longest x4 46.9 us: on_device(): pieces = forecast(info, own, near, far, w1, b1, w2, b2)]
    all_gather x2 -> x1, blocking collectives: 131 us -> 70.8 us  [on_device(): gathered = lax.all_gather(packed, ('grp', 'band'), axis=0)]
    all_to_all x1 -> x0, waiting for transfers between devices: 48.1 us -> none  [on_device(): lax.all_to_all(predicted_samples, 'grp', split_axis=3, concat_axis=0, til...]
    squeeze x24 -> x0, local copies, waits for them, and re-layouts: 29.4 us -> none  [the longest x16 20.6 us: on_device(): lax.map(output_layer, (prior_samples, hidden_fields, northern_halo, south...]
    ppermute x4 -> x20, starting transfers between devices: 15.2 us -> 31 us  [the longest x4 17.5 us: on_device(): far = lax.ppermute(near, 'band', forward)]
  transfers between devices with their start and end apart: 6 -> 20, of which waited for: 3 -> 8; matrix products, arithmetic and copies ran while one was open for 1% -> 2% of each run, Pallas kernels for 0% -> 22%
where the time goes in v1:
time: 213 us
  blocking collectives  70.8 us (33%)
  Pallas kernels  62.1 us (29%)
  waiting for transfers between devices  42.3 us (20%)
  starting transfers between devices  31 us (15%)
  local copies, waits for them, and re-layouts  6.33 us (3%)
    all_gather x1, blocking collectives, on_device(): gathered = lax.all_gather(packed, ('grp', 'band'), axis=0)  70.8 us
    pallas_call x4, Pallas kernels, on_device(): pieces = forecast(info, own, near, far, w1, b1, w2, b2)  46.9 us
    ppermute x4, waiting for transfers between devices, on_device(): near = lax.ppermute(own, 'band', swap)  31.7 us
    ppermute x4, starting transfers between devices, on_device(): far = lax.ppermute(near, 'band', forward)  17.5 us
    ppermute x12, waiting for transfers between devices, on_device(): piece = lax.ppermute(piece, 'grp', [(i, i ^ step) for i in range(groups)])  10.5 us
    pallas_call x1, Pallas kernels, on_device(): pl.pallas_call(functools.partial(analysis_kernel, members=members, chans=...  8.43 us
    ppermute x12, starting transfers between devices, on_device(): piece = lax.ppermute(piece, 'grp', [(i, i ^ step) for i in range(groups)])  8.25 us
    pallas_call x1, Pallas kernels, on_device(): pl.pallas_call(functools.partial(gram_kernel, pairs=pairs, groups=groups,...  6.78 us
  transfers between devices with their start and end apart: 20, of which 8 were waited for; matrix products, arithmetic and copies ran while one was open for 2% of the time, Pallas kernels for 22%

profile of v1, /device:TPU:0, one launch (start us, length us, event | category | flops | bytes accessed | tf_op | source)
XLA Modules:
  0.0 213.1 jit_solution(16580165512596281448)
XLA Ops:
  0.0 2.8 %fusion.4 = (bf16[2,69,2,1024]{3,2,1,0:T(2,128)(2,1)S(1)}, bf16[2,69,2,1024]{3,2,1,0:T(2,128)(2,1)S(1)}, bf16[2,69,2,1024]{3,2,1,0:T(2,128)(2,1)S(1)}, bf16[2,69,2,1024]{3,2,1,0:T(2,128)(2,1)S(1)}) fusion(bf16[8,69,2,1024]{3,2,1,0:T(2,128)(2,1)} %param.10), kind=kLoop, calls=%fused_computation.18 | loop fusion | bytes 4521984 | tf_op jit(solution)/shard_map/slice | solution.py:248
  3.0 3.0 %collective-permute-start = (bf16[2,2,72,1024]{3,2,1,0:T(8,128)(2,1)S(1)}, bf16[2,2,72,1024]{3,2,1,0:T(8,128)(2,1)}, u32[]{:S(2)}, u32[]{:S(2)}) collective-permute-start(bf16[2,2,72,1024]{3,2,1,0:T(8,128)(2,1)S(1)} %pad.29.own), channel_id=1, source_target_pairs={{0,1},{1,0},{2,3},{3,2},{4,5},{5,4},{6,7},{7,6},{8,9},{9,8},{10,11... | collective-permute-start | bytes 1769480 | tf_op jit(solution)/shard_map/ppermute | solution.py:250
  6.6 2.1 collective-permute-start.10
  8.9 11.4 %collective-permute-done.near = bf16[2,2,72,1024]{3,2,1,0:T(8,128)(2,1)} collective-permute-done((bf16[2,2,72,1024]{3,2,1,0:T(8,128)(2,1)S(1)}, bf16[2,2,72,1024]{3,2,1,0:T(8,128)(2,1)}, u32[]{:S(2)}, u32[]{:S(2)}) %collective-permute-start) | collective-permute-done | bytes 589856 | tf_op jit(solution)/shard_map/ppermute | solution.py:250
  20.3 4.9 %collective-permute-start.1 = (bf16[2,2,72,1024]{3,2,1,0:T(8,128)(2,1)}, bf16[2,2,72,1024]{3,2,1,0:T(8,128)(2,1)}, u32[]{:S(2)}, u32[]{:S(2)}) collective-permute-start(bf16[2,2,72,1024]{3,2,1,0:T(8,128)(2,1)} %collective-permute-done.near), channel_id=1, source_target_pairs={{3,1},{5,3},{7,5},{0,2},{2,4},{4,6},{11,9},{13,11},{15,13},{8,10},... | collective-permute-start | bytes 1769480 | tf_op jit(solution)/shard_map/ppermute | solution.py:251
  25.2 0.8 pad_bitcast_fusion
  25.9 7.0 %collective-permute-done.5.near = bf16[2,2,72,1024]{3,2,1,0:T(8,128)(2,1)} collective-permute-done((bf16[2,2,72,1024]{3,2,1,0:T(8,128)(2,1)S(1)}, bf16[2,2,72,1024]{3,2,1,0:T(8,128)(2,1)}, u32[]{:S(2)}, u32[]{:S(2)}) %collective-permute-start.5) | collective-permute-done | bytes 589856 | tf_op jit(solution)/shard_map/ppermute | solution.py:250
  32.9 4.9 %collective-permute-start.6 = (bf16[2,2,72,1024]{3,2,1,0:T(8,128)(2,1)}, bf16[2,2,72,1024]{3,2,1,0:T(8,128)(2,1)}, u32[]{:S(2)}, u32[]{:S(2)}) collective-permute-start(bf16[2,2,72,1024]{3,2,1,0:T(8,128)(2,1)} %collective-permute-done.5.near), channel_id=1, source_target_pairs={{3,1},{5,3},{7,5},{0,2},{2,4},{4,6},{11,9},{13,11},{15,13},{8,10},... | collective-permute-start | bytes 1769480 | tf_op jit(solution)/shard_map/ppermute | solution.py:251
  38.6 1.1 copy.30
  39.9 5.6 %collective-permute-done.10.near = bf16[2,2,72,1024]{3,2,1,0:T(8,128)(2,1)} collective-permute-done((bf16[2,2,72,1024]{3,2,1,0:T(8,128)(2,1)S(1)}, bf16[2,2,72,1024]{3,2,1,0:T(8,128)(2,1)}, u32[]{:S(2)}, u32[]{:S(2)}) %collective-permute-start.10) | collective-permute-done | bytes 589856 | tf_op jit(solution)/shard_map/ppermute | solution.py:250
  45.6 4.1 %collective-permute-start.11 = (bf16[2,2,72,1024]{3,2,1,0:T(8,128)(2,1)}, bf16[2,2,72,1024]{3,2,1,0:T(8,128)(2,1)S(1)}, u32[]{:S(2)}, u32[]{:S(2)}) collective-permute-start(bf16[2,2,72,1024]{3,2,1,0:T(8,128)(2,1)} %collective-permute-done.10.near), channel_id=1, source_target_pairs={{3,1},{5,3},{7,5},{0,2},{2,4},{4,6},{11,9},{13,11},{15,13},{8,10},... | collective-permute-start | bytes 1769480 | tf_op jit(solution)/shard_map/ppermute | solution.py:251
  49.6 7.7 %collective-permute-done.15.near = bf16[2,2,72,1024]{3,2,1,0:T(8,128)(2,1)} collective-permute-done((bf16[2,2,72,1024]{3,2,1,0:T(8,128)(2,1)S(1)}, bf16[2,2,72,1024]{3,2,1,0:T(8,128)(2,1)}, u32[]{:S(2)}, u32[]{:S(2)}) %collective-permute-start.15) | collective-permute-done | bytes 589856 | tf_op jit(solution)/shard_map/ppermute | solution.py:250
  57.4 3.8 %collective-permute-start.16 = (bf16[2,2,72,1024]{3,2,1,0:T(8,128)(2,1)}, bf16[2,2,72,1024]{3,2,1,0:T(8,128)(2,1)S(1)}, u32[]{:S(2)}, u32[]{:S(2)}) collective-permute-start(bf16[2,2,72,1024]{3,2,1,0:T(8,128)(2,1)} %collective-permute-done.15.near), channel_id=1, source_target_pairs={{3,1},{5,3},{7,5},{0,2},{2,4},{4,6},{11,9},{13,11},{15,13},{8,10},... | collective-permute-start | bytes 1769480 | tf_op jit(solution)/shard_map/ppermute | solution.py:251
  61.2 11.8 %forecast.4 = (bf16[2,144,256]{2,1,0:T(8,128)(2,1)S(1)}, bf16[2,144,256]{2,1,0:T(8,128)(2,1)S(1)}, bf16[2,144,256]{2,1,0:T(8,128)(2,1)S(1)}, bf16[2,144,256]{2,1,0:T(8,128)(2,1)S(1)}) custom-call(s32[4]{0:T(128)S(1)} %pad_add_fusion.info, bf16[2,2,72,1024]{3,2,1,0:T(8,128)(2,1)S(1)} %pad.29.own, bf16[2,2,72,1024]{3,2,1,0:T(8,128)(2,1)} %collective-permute-done.near, ...), custom_call_target="tpu_custom_call" | custom-call | flops 4831838208 | bytes 4194304 | tf_op jit(solution)/shard_map/forecast/pallas_call | solution.py:252
  73.1 1.6 collective-permute-start.3
  74.7 0.3 collective-permute-start.4
  74.9 11.7 %forecast.5 = (bf16[2,144,256]{2,1,0:T(8,128)(2,1)S(1)}, bf16[2,144,256]{2,1,0:T(8,128)(2,1)S(1)}, bf16[2,144,256]{2,1,0:T(8,128)(2,1)S(1)}, bf16[2,144,256]{2,1,0:T(8,128)(2,1)S(1)}) custom-call(s32[4]{0:T(128)S(1)} %pad_add_fusion.info, bf16[2,2,72,1024]{3,2,1,0:T(8,128)(2,1)S(1)} %pad.34.own, bf16[2,2,72,1024]{3,2,1,0:T(8,128)(2,1)} %collective-permute-done.5.near, ...), custom_call_target="tpu_custom_call" | custom-call | flops 4831838208 | bytes 4194304 | tf_op jit(solution)/shard_map/forecast/pallas_call | solution.py:252
  86.6 0.4 collective-permute-start.7
  87.0 11.7 %forecast.6 = (bf16[2,144,256]{2,1,0:T(8,128)(2,1)S(1)}, bf16[2,144,256]{2,1,0:T(8,128)(2,1)S(1)}, bf16[2,144,256]{2,1,0:T(8,128)(2,1)S(1)}, bf16[2,144,256]{2,1,0:T(8,128)(2,1)S(1)}) custom-call(s32[4]{0:T(128)S(1)} %pad_add_fusion.info, bf16[2,2,72,1024]{3,2,1,0:T(8,128)(2,1)S(1)} %pad.35.own, bf16[2,2,72,1024]{3,2,1,0:T(8,128)(2,1)} %collective-permute-done.10.near, ...), custom_call_target="tpu_custom_call" | custom-call | flops 4831838208 | bytes 4194304 | tf_op jit(solution)/shard_map/forecast/pallas_call | solution.py:252
  98.7 1.6 collective-permute-start.8
  100.3 0.6 collective-permute-start.12
  100.9 11.8 %forecast.7 = (bf16[2,144,256]{2,1,0:T(8,128)(2,1)S(1)}, bf16[2,144,256]{2,1,0:T(8,128)(2,1)S(1)}, bf16[2,144,256]{2,1,0:T(8,128)(2,1)S(1)}, bf16[2,144,256]{2,1,0:T(8,128)(2,1)S(1)}) custom-call(s32[4]{0:T(128)S(1)} %pad_add_fusion.info, bf16[2,2,72,1024]{3,2,1,0:T(8,128)(2,1)S(1)} %pad.36.own, bf16[2,2,72,1024]{3,2,1,0:T(8,128)(2,1)} %collective-permute-done.15.near, ...), custom_call_target="tpu_custom_call" | custom-call | flops 4831838208 | bytes 4194304 | tf_op jit(solution)/shard_map/forecast/pallas_call | solution.py:252
  112.7 1.6 collective-permute-start.13
  114.3 0.6 collective-permute-start.17
  114.9 1.5 collective-permute-start.18
  116.6 2.9 %collective-permute-done.13.rest_10_ = bf16[2,144,256]{2,1,0:T(8,128)(2,1)S(1)} collective-permute-done((bf16[2,144,256]{2,1,0:T(8,128)(2,1)S(1)}, bf16[2,144,256]{2,1,0:T(8,128)(2,1)S(1)}, u32[]{:S(2)}, u32[]{:S(2)}) %collective-permute-start.13) | collective-permute-done | bytes 147488 | tf_op jit(solution)/shard_map/ppermute | solution.py:256
  119.5 2.2 %collective-permute-done.14.rest_11_ = bf16[2,144,256]{2,1,0:T(8,128)(2,1)S(1)} collective-permute-done((bf16[2,144,256]{2,1,0:T(8,128)(2,1)S(1)}, bf16[2,144,256]{2,1,0:T(8,128)(2,1)S(1)}, u32[]{:S(2)}, u32[]{:S(2)}) %collective-permute-start.14) | collective-permute-done | bytes 147488 | tf_op jit(solution)/shard_map/ppermute | solution.py:256
  121.7 4.1 %collective-permute-done.18.rest_14_ = bf16[2,144,256]{2,1,0:T(8,128)(2,1)S(1)} collective-permute-done((bf16[2,144,256]{2,1,0:T(8,128)(2,1)S(1)}, bf16[2,144,256]{2,1,0:T(8,128)(2,1)S(1)}, u32[]{:S(2)}, u32[]{:S(2)}) %collective-permute-start.18) | collective-permute-done | bytes 147488 | tf_op jit(solution)/shard_map/ppermute | solution.py:256
  125.8 1.3 collective-permute-done.19.rest_15_
  127.1 6.8 %grams.1 = (bf16[2,9,256,256]{3,2,1,0:T(8,128)(2,1)S(1)}, f32[32,128]{1,0:T(8,128)S(1)}) custom-call(s32[4]{0:T(128)S(1)} %pad_add_fusion.info, bf16[2,144,256]{2,1,0:T(8,128)(2,1)S(1)} %get-tuple-element.23.rest_0_, bf16[2,144,256]{2,1,0:T(8,128)(2,1)S(1)} %collective-permute-done.2.rest_1_, bf16[2,144,256]{2,1,0:T(8,128)(2,1)S(1)} %collective-permute-done.3.rest_2_, ...), custom_call_target="tpu_custom_call" | custom-call | tf_op jit(solution)/shard_map/grams/pallas_call | solution.py:261
  133.9 70.8 %all-gather = f32[1024,128]{1,0:T(8,128)S(1)} all-gather(f32[32,128]{1,0:T(8,128)S(1)} %get-tuple-element.39.mine), channel_id=2, replica_groups=mesh['grp'=4,'band'=8] {'grp','band'}, dimensions={0}, use_global_device_ids=true | all-gather | bytes 540672 | tf_op jit(solution)/shard_map/all_gather | solution.py:281
  204.7 8.4 %analyse.1 = f32[8832,128]{1,0:T(8,128)} custom-call(s32[2,8]{1,0:T(2,128)S(1)} %copy-done.2, f32[2,8]{1,0:T(2,128)S(1)} %copy-done.3, f32[32,128]{1,0:T(8,128)S(1)} %get-tuple-element.39.mine, f32[32,32,128]{2,1,0:T(8,128)S(1)} %bitcast.38, bf16[2,9,256,256]{3,2,1,0:T(8,128)(2,1)S(1)} %get-tuple-element.40.field), custom_call_target="tpu_custom_call" | custom-call | tf_op jit(solution)/shard_map/analyse/pallas_call | solution.py:282
  (56 shorter events, 2.1 us)
Async XLA Ops:
  3.0 17.3 %collective-permute-start = (bf16[2,2,72,1024]{3,2,1,0:T(8,128)(2,1)S(1)}, bf16[2,2,72,1024]{3,2,1,0:T(8,128)(2,1)}, u32[]{:S(2)}, u32[]{:S(2)}) collective-permute-start(bf16[2,2,72,1024]{3,2,1,0:T(8,128)(2,1)S(1)} %pad.29.own), channel_id=1, source_target_pairs={{0,1},{1,0},{2,3},{3,2},{4,5},{5,4},{6,7},{7,6},{8,9},{9,8},{10,11... | collective-permute-start | bytes 1769480 | tf_op jit(solution)/shard_map/ppermute | solution.py:250
  6.2 18.9 %copy-start.5 = (bf16[3,3,69,256]{3,2,1,0:T(8,128)(2,1)S(1)}, bf16[3,3,69,256]{3,2,1,0:T(8,128)(2,1)}, u32[]{:S(2)}) copy-start(bf16[3,3,69,256]{3,2,1,0:T(8,128)(2,1)} %param.13) | copy-start | bytes 953860
  6.2 26.7 %collective-permute-start.5 = (bf16[2,2,72,1024]{3,2,1,0:T(8,128)(2,1)S(1)}, bf16[2,2,72,1024]{3,2,1,0:T(8,128)(2,1)}, u32[]{:S(2)}, u32[]{:S(2)}) collective-permute-start(bf16[2,2,72,1024]{3,2,1,0:T(8,128)(2,1)S(1)} %pad.34.own), channel_id=1, source_target_pairs={{0,1},{1,0},{2,3},{3,2},{4,5},{5,4},{6,7},{7,6},{8,9},{9,8},{10,11... | collective-permute-start | bytes 1769480 | tf_op jit(solution)/shard_map/ppermute | solution.py:250
  6.5 19.4 %copy-start.6 = (s32[2,256]{1,0:T(2,128)S(1)}, s32[2,256]{1,0:T(2,128)}, u32[]{:S(2)}) copy-start(s32[2,256]{1,0:T(2,128)} %param.15) | copy-start | bytes 6148
  6.5 31.3 %copy-start.8 = (f32[69]{0:T(128)S(1)}, f32[69]{0:T(128)}, u32[]{:S(2)}) copy-start(f32[69]{0:T(128)} %param.14) | copy-start | bytes 832
  6.5 31.7 %copy-start.7 = (f32[256]{0:T(256)S(1)}, f32[256]{0:T(256)}, u32[]{:S(2)}) copy-start(f32[256]{0:T(256)} %param.12) | copy-start | bytes 3076
  6.5 31.9 %copy-start.4 = (bf16[3,3,256,69]{2,3,1,0:T(8,128)(2,1)S(1)}, bf16[3,3,256,69]{2,3,1,0:T(8,128)(2,1)}, u32[]{:S(2)}) copy-start(bf16[3,3,256,69]{2,3,1,0:T(8,128)(2,1)} %param.11) | copy-start | bytes 953860
  6.6 39.0 %collective-permute-start.10 = (bf16[2,2,72,1024]{3,2,1,0:T(8,128)(2,1)S(1)}, bf16[2,2,72,1024]{3,2,1,0:T(8,128)(2,1)}, u32[]{:S(2)}, u32[]{:S(2)}) collective-permute-start(bf16[2,2,72,1024]{3,2,1,0:T(8,128)(2,1)S(1)} %pad.35.own), channel_id=1, source_target_pairs={{0,1},{1,0},{2,3},{3,2},{4,5},{5,4},{6,7},{7,6},{8,9},{9,8},{10,11... | collective-permute-start | bytes 1769480 | tf_op jit(solution)/shard_map/ppermute | solution.py:250
  8.8 48.5 %collective-permute-start.15 = (bf16[2,2,72,1024]{3,2,1,0:T(8,128)(2,1)S(1)}, bf16[2,2,72,1024]{3,2,1,0:T(8,128)(2,1)}, u32[]{:S(2)}, u32[]{:S(2)}) collective-permute-start(bf16[2,2,72,1024]{3,2,1,0:T(8,128)(2,1)S(1)} %pad.36.own), channel_id=1, source_target_pairs={{0,1},{1,0},{2,3},{3,2},{4,5},{5,4},{6,7},{7,6},{8,9},{9,8},{10,11... | collective-permute-start | bytes 1769480 | tf_op jit(solution)/shard_map/ppermute | solution.py:250
  20.3 40.9 %collective-permute-start.1 = (bf16[2,2,72,1024]{3,2,1,0:T(8,128)(2,1)}, bf16[2,2,72,1024]{3,2,1,0:T(8,128)(2,1)}, u32[]{:S(2)}, u32[]{:S(2)}) collective-permute-start(bf16[2,2,72,1024]{3,2,1,0:T(8,128)(2,1)} %collective-permute-done.near), channel_id=1, source_target_pairs={{3,1},{5,3},{7,5},{0,2},{2,4},{4,6},{11,9},{13,11},{15,13},{8,10},... | collective-permute-start | bytes 1769480 | tf_op jit(solution)/shard_map/ppermute | solution.py:251
  32.9 41.7 %collective-permute-start.6 = (bf16[2,2,72,1024]{3,2,1,0:T(8,128)(2,1)}, bf16[2,2,72,1024]{3,2,1,0:T(8,128)(2,1)}, u32[]{:S(2)}, u32[]{:S(2)}) collective-permute-start(bf16[2,2,72,1024]{3,2,1,0:T(8,128)(2,1)} %collective-permute-done.5.near), channel_id=1, source_target_pairs={{3,1},{5,3},{7,5},{0,2},{2,4},{4,6},{11,9},{13,11},{15,13},{8,10},... | collective-permute-start | bytes 1769480 | tf_op jit(solution)/shard_map/ppermute | solution.py:251
  45.6 41.0 %collective-permute-start.11 = (bf16[2,2,72,1024]{3,2,1,0:T(8,128)(2,1)}, bf16[2,2,72,1024]{3,2,1,0:T(8,128)(2,1)S(1)}, u32[]{:S(2)}, u32[]{:S(2)}) collective-permute-start(bf16[2,2,72,1024]{3,2,1,0:T(8,128)(2,1)} %collective-permute-done.10.near), channel_id=1, source_target_pairs={{3,1},{5,3},{7,5},{0,2},{2,4},{4,6},{11,9},{13,11},{15,13},{8,10},... | collective-permute-start | bytes 1769480 | tf_op jit(solution)/shard_map/ppermute | solution.py:251
  57.4 41.3 %collective-permute-start.16 = (bf16[2,2,72,1024]{3,2,1,0:T(8,128)(2,1)}, bf16[2,2,72,1024]{3,2,1,0:T(8,128)(2,1)S(1)}, u32[]{:S(2)}, u32[]{:S(2)}) collective-permute-start(bf16[2,2,72,1024]{3,2,1,0:T(8,128)(2,1)} %collective-permute-done.15.near), channel_id=1, source_target_pairs={{3,1},{5,3},{7,5},{0,2},{2,4},{4,6},{11,9},{13,11},{15,13},{8,10},... | collective-permute-start | bytes 1769480 | tf_op jit(solution)/shard_map/ppermute | solution.py:251
  73.0 27.3 %collective-permute-start.2 = (bf16[2,144,256]{2,1,0:T(8,128)(2,1)S(1)}, bf16[2,144,256]{2,1,0:T(8,128)(2,1)S(1)}, u32[]{:S(2)}, u32[]{:S(2)}) collective-permute-start(bf16[2,144,256]{2,1,0:T(8,128)(2,1)S(1)} %get-tuple-element.24), channel_id=1, source_target_pairs={{0,8},{8,0},{16,24},{24,16},{1,9},{9,1},{17,25},{25,17},{2,10},{10... | collective-permute-start | bytes 442376 | tf_op jit(solution)/shard_map/ppermute | solution.py:256
  73.1 27.3 %collective-permute-start.3 = (bf16[2,144,256]{2,1,0:T(8,128)(2,1)S(1)}, bf16[2,144,256]{2,1,0:T(8,128)(2,1)S(1)}, u32[]{:S(2)}, u32[]{:S(2)}) collective-permute-start(bf16[2,144,256]{2,1,0:T(8,128)(2,1)S(1)} %get-tuple-element.25), channel_id=1, source_target_pairs={{0,16},{8,24},{16,0},{24,8},{1,17},{9,25},{17,1},{25,9},{2,18},{10... | collective-permute-start | bytes 442376 | tf_op jit(solution)/shard_map/ppermute | solution.py:256
  74.7 38.0 %collective-permute-start.4 = (bf16[2,144,256]{2,1,0:T(8,128)(2,1)S(1)}, bf16[2,144,256]{2,1,0:T(8,128)(2,1)S(1)}, u32[]{:S(2)}, u32[]{:S(2)}) collective-permute-start(bf16[2,144,256]{2,1,0:T(8,128)(2,1)S(1)} %get-tuple-element.26), channel_id=1, source_target_pairs={{0,24},{8,16},{16,8},{24,0},{1,25},{9,17},{17,9},{25,1},{2,26},{10... | collective-permute-start | bytes 442376 | tf_op jit(solution)/shard_map/ppermute | solution.py:256
  86.6 27.7 %collective-permute-start.7 = (bf16[2,144,256]{2,1,0:T(8,128)(2,1)S(1)}, bf16[2,144,256]{2,1,0:T(8,128)(2,1)S(1)}, u32[]{:S(2)}, u32[]{:S(2)}) collective-permute-start(bf16[2,144,256]{2,1,0:T(8,128)(2,1)S(1)} %get-tuple-element.28), channel_id=1, source_target_pairs={{0,8},{8,0},{16,24},{24,16},{1,9},{9,1},{17,25},{25,17},{2,10},{10... | collective-permute-start | bytes 442376 | tf_op jit(solution)/shard_map/ppermute | solution.py:256
  98.7 15.6 %collective-permute-start.8 = (bf16[2,144,256]{2,1,0:T(8,128)(2,1)S(1)}, bf16[2,144,256]{2,1,0:T(8,128)(2,1)S(1)}, u32[]{:S(2)}, u32[]{:S(2)}) collective-permute-start(bf16[2,144,256]{2,1,0:T(8,128)(2,1)S(1)} %get-tuple-element.29), channel_id=1, source_target_pairs={{0,16},{8,24},{16,0},{24,8},{1,17},{9,25},{17,1},{25,9},{2,18},{10... | collective-permute-start | bytes 442376 | tf_op jit(solution)/shard_map/ppermute | solution.py:256
  100.3 14.6 %collective-permute-start.9 = (bf16[2,144,256]{2,1,0:T(8,128)(2,1)S(1)}, bf16[2,144,256]{2,1,0:T(8,128)(2,1)S(1)}, u32[]{:S(2)}, u32[]{:S(2)}) collective-permute-start(bf16[2,144,256]{2,1,0:T(8,128)(2,1)S(1)} %get-tuple-element.30), channel_id=1, source_target_pairs={{0,24},{8,16},{16,8},{24,0},{1,25},{9,17},{17,9},{25,1},{2,26},{10... | collective-permute-start | bytes 442376 | tf_op jit(solution)/shard_map/ppermute | solution.py:256
  100.3 26.8 %copy-start = (f32[2,256]{1,0:T(2,128)S(1)}, f32[2,256]{1,0:T(2,128)}, u32[]{:S(2)}) copy-start(f32[2,256]{1,0:T(2,128)} %rest_18_.1) | copy-start | bytes 6148
  100.3 26.8 %copy-start.1 = (f32[2,256]{1,0:T(2,128)S(1)}, f32[2,256]{1,0:T(2,128)}, u32[]{:S(2)}) copy-start(f32[2,256]{1,0:T(2,128)} %rest_19_.1) | copy-start | bytes 6148
  100.3 16.1 %collective-permute-start.12 = (bf16[2,144,256]{2,1,0:T(8,128)(2,1)S(1)}, bf16[2,144,256]{2,1,0:T(8,128)(2,1)S(1)}, u32[]{:S(2)}, u32[]{:S(2)}) collective-permute-start(bf16[2,144,256]{2,1,0:T(8,128)(2,1)S(1)} %get-tuple-element.32), channel_id=1, source_target_pairs={{0,8},{8,0},{16,24},{24,16},{1,9},{9,1},{17,25},{25,17},{2,10},{10... | collective-permute-start | bytes 442376 | tf_op jit(solution)/shard_map/ppermute | solution.py:256
  112.7 92.0 %copy-start.2 = (s32[2,8]{1,0:T(2,128)S(1)}, s32[2,8]{1,0:T(2,128)}, u32[]{:S(2)}) copy-start(s32[2,8]{1,0:T(2,128)} %neighbours.1) | copy-start | bytes 196
  112.7 92.0 %copy-start.3 = (f32[2,8]{1,0:T(2,128)S(1)}, f32[2,8]{1,0:T(2,128)}, u32[]{:S(2)}) copy-start(f32[2,8]{1,0:T(2,128)} %weights.1) | copy-start | bytes 196
  112.7 6.8 %collective-permute-start.13 = (bf16[2,144,256]{2,1,0:T(8,128)(2,1)S(1)}, bf16[2,144,256]{2,1,0:T(8,128)(2,1)S(1)}, u32[]{:S(2)}, u32[]{:S(2)}) collective-permute-start(bf16[2,144,256]{2,1,0:T(8,128)(2,1)S(1)} %get-tuple-element.33), channel_id=1, source_target_pairs={{0,16},{8,24},{16,0},{24,8},{1,17},{9,25},{17,1},{25,9},{2,18},{10... | collective-permute-start | bytes 442376 | tf_op jit(solution)/shard_map/ppermute | solution.py:256
  114.3 7.4 %collective-permute-start.14 = (bf16[2,144,256]{2,1,0:T(8,128)(2,1)S(1)}, bf16[2,144,256]{2,1,0:T(8,128)(2,1)S(1)}, u32[]{:S(2)}, u32[]{:S(2)}) collective-permute-start(bf16[2,144,256]{2,1,0:T(8,128)(2,1)S(1)} %get-tuple-element.34), channel_id=1, source_target_pairs={{0,24},{8,16},{16,8},{24,0},{1,25},{9,17},{17,9},{25,1},{2,26},{10... | collective-permute-start | bytes 442376 | tf_op jit(solution)/shard_map/ppermute | solution.py:256
  114.3 7.4 %collective-permute-start.17 = (bf16[2,144,256]{2,1,0:T(8,128)(2,1)S(1)}, bf16[2,144,256]{2,1,0:T(8,128)(2,1)S(1)}, u32[]{:S(2)}, u32[]{:S(2)}) collective-permute-start(bf16[2,144,256]{2,1,0:T(8,128)(2,1)S(1)} %get-tuple-element.36), channel_id=1, source_target_pairs={{0,8},{8,0},{16,24},{24,16},{1,9},{9,1},{17,25},{25,17},{2,10},{10... | collective-permute-start | bytes 442376 | tf_op jit(solution)/shard_map/ppermute | solution.py:256
  114.9 10.9 %collective-permute-start.18 = (bf16[2,144,256]{2,1,0:T(8,128)(2,1)S(1)}, bf16[2,144,256]{2,1,0:T(8,128)(2,1)S(1)}, u32[]{:S(2)}, u32[]{:S(2)}) collective-permute-start(bf16[2,144,256]{2,1,0:T(8,128)(2,1)S(1)} %get-tuple-element.37), channel_id=1, source_target_pairs={{0,16},{8,24},{16,0},{24,8},{1,17},{9,25},{17,1},{25,9},{2,18},{10... | collective-permute-start | bytes 442376 | tf_op jit(solution)/shard_map/ppermute | solution.py:256
  116.5 10.6 %collective-permute-start.19 = (bf16[2,144,256]{2,1,0:T(8,128)(2,1)S(1)}, bf16[2,144,256]{2,1,0:T(8,128)(2,1)S(1)}, u32[]{:S(2)}, u32[]{:S(2)}) collective-permute-start(bf16[2,144,256]{2,1,0:T(8,128)(2,1)S(1)} %get-tuple-element.38), channel_id=1, source_target_pairs={{0,24},{8,16},{16,8},{24,0},{1,25},{9,17},{17,9},{25,1},{2,26},{10... | collective-permute-start | bytes 442376 | tf_op jit(solution)/shard_map/ppermute | solution.py:256

commit v2 on v1

--- a/solution.py
+++ b/solution.py
@@ -12,6 +12,7 @@
 ROWK = 224
 SMEM = pl.BlockSpec(memory_space=pltpu.SMEM)
 VMEM = pl.BlockSpec(memory_space=pltpu.VMEM)
+MESH = pl.DeviceIdType.MESH
 HIGH = lax.Precision.HIGHEST
 
 
@@ -78,10 +79,57 @@
             outs[step][row] = block.reshape(chans * PAIR, width).astype(jnp.bfloat16)
 
 
-def gram_kernel(info, *rest, pairs, groups, chans, members, nobs, width):
+def exchange_start(bands, groups):
+    grp, band = lax.axis_index("grp"), lax.axis_index("band")
+    barrier = pltpu.get_barrier_semaphore()
+    for step in range(1, bands):
+        peer = lax.rem(band + step, bands)
+        pl.semaphore_signal(barrier, inc=1, device_id={"band": peer}, device_id_type=MESH)
+    for step in range(1, groups):
+        peer = jnp.bitwise_xor(grp, step)
+        pl.semaphore_signal(barrier, inc=1, device_id={"grp": peer}, device_id_type=MESH)
+
+
+def exchange_all(gathered, bands, groups, band_sems, grp_sems):
+    grp, band = lax.axis_index("grp"), lax.axis_index("band")
+    pl.semaphore_wait(pltpu.get_barrier_semaphore(), bands + groups - 2)
+    first = [
+        pltpu.make_async_remote_copy(
+            src_ref=gathered.at[grp, band],
+            dst_ref=gathered.at[grp, band],
+            send_sem=band_sems.at[0, step],
+            recv_sem=band_sems.at[1, step],
+            device_id={"band": lax.rem(band + step, bands)},
+            device_id_type=MESH,
+        )
+        for step in range(1, bands)
+    ]
+    for copy in first:
+        copy.start()
+    for copy in first:
+        copy.wait()
+    second = [
+        pltpu.make_async_remote_copy(
+            src_ref=gathered.at[grp],
+            dst_ref=gathered.at[grp],
+            send_sem=grp_sems.at[0, step],
+            recv_sem=grp_sems.at[1, step],
+            device_id={"grp": jnp.bitwise_xor(grp, step)},
+            device_id_type=MESH,
+        )
+        for step in range(1, groups)
+    ]
+    for copy in second:
+        copy.start()
+    for copy in second:
+        copy.wait()
+
+
+def gram_kernel(*rest, pairs, bands, groups, chans, members, nobs, width):
     slabs = rest[: groups * pairs]
-    chan, col, obs, prec, field, packed, pred = rest[groups * pairs :]
-    grp = info[1]
+    chan, col, obs, prec, field, packed, gathered, pred, band_sems, grp_sems = rest[groups * pairs :]
+    exchange_start(bands, groups)
+    grp = lax.axis_index("grp")
     blocks = chans // 8
     depth = chans * PAIR
     lane = lax.broadcasted_iota(jnp.int32, (nobs, depth), 1)
@@ -125,6 +173,8 @@
             precision=HIGH,
             preferred_element_type=jnp.float32,
         )
+    gathered[grp, lax.axis_index("band")] = packed[...]
+    exchange_all(gathered, bands, groups, band_sems, grp_sems)
 
 
 def analysis_kernel(neighbours, weights, mine, gathered, field, out, *, members, chans, real, width):
@@ -150,7 +200,8 @@
         total = mine[...] if row == 0 else pltpu.roll(mine[...], 64, 1)
         for k in range(neighbours.shape[1]):
             j = neighbours[row, k]
-            gram = gathered[j // 2]
+            bands = gathered.shape[1]
+            gram = gathered[j // (2 * bands), (j // 2) % bands]
             gram = jnp.where(j % 2 == 1, pltpu.roll(gram, 64, 1), gram)
             total = total + weights[row, k] * gram
         matrix = total[:, :members] + (members - 1.0) * eye
@@ -248,6 +299,8 @@
         own = prior_samples[pair * PAIR : (pair + 1) * PAIR]
         own = jnp.pad(jnp.transpose(own, (0, 2, 1, 3)), ((0, 0), (0, 0), (0, chans - real), (0, 0)))
         near = lax.ppermute(own, "band", swap)
+        if pair >= 2:
+            near, _ = lax.optimization_barrier((near, slabs[(pair - 2) * groups]))
         far = lax.ppermute(near, "band", forward)
         pieces = forecast(info, own, near, far, w1, b1, w2, b2)
         for step in range(groups):
@@ -258,10 +311,11 @@
 
     chan = (obs_index // width).T
     col = (obs_index % width).T
-    field, packed = pl.pallas_call(
+    field, packed, gathered = pl.pallas_call(
         functools.partial(
             gram_kernel,
             pairs=pairs,
+            bands=bands,
             groups=groups,
             chans=chans,
             members=members,
@@ -271,14 +325,20 @@
         out_shape=[
             jax.ShapeDtypeStruct((height, chans // 8, members * 8, width), jnp.bfloat16),
             jax.ShapeDtypeStruct((members, 128), jnp.float32),
+            jax.ShapeDtypeStruct((groups, bands, members, 128), jnp.float32),
         ],
-        in_specs=[SMEM] + [VMEM] * (len(slabs) + 4),
-        out_specs=[VMEM] * 2,
-        scratch_shapes=[pltpu.VMEM((members, 8, nobs), jnp.float32)],
-        compiler_params=pltpu.CompilerParams(vmem_limit_bytes=40 * 2**20),
+        in_specs=[VMEM] * (len(slabs) + 4),
+        out_specs=[VMEM] * 3,
+        scratch_shapes=[
+            pltpu.VMEM((members, 8, nobs), jnp.float32),
+            pltpu.SemaphoreType.DMA((2, bands)),
+            pltpu.SemaphoreType.DMA((2, groups)),
+        ],
+        compiler_params=pltpu.CompilerParams(
+            vmem_limit_bytes=40 * 2**20, collective_id=1, has_side_effects=True
+        ),
         name="grams",
-    )(info, *slabs, chan, col, obs_values, obs_prec)
-    gathered = lax.all_gather(packed, ("grp", "band"), axis=0)
+    )(*slabs, chan, col, obs_values, obs_prec)
     out = pl.pallas_call(
         functools.partial(analysis_kernel, members=members, chans=chans, real=real, width=width),
         out_shape=jax.ShapeDtypeStruct((members * real * 2 * height, 128), jnp.float32),

time: 213 us -> 141 us (0.66)
  blocking collectives: 70.8 us -> 0 us
  waiting for transfers between devices: 42.3 us -> 28.9 us
  Pallas kernels: 62.1 us -> 73.6 us
    all_gather x1 -> x0, blocking collectives: 70.8 us -> none  [on_device(): gathered = lax.all_gather(packed, ('grp', 'band'), axis=0)]
    ppermute x4, waiting for transfers between devices: 31.7 us -> 18.4 us  [on_device(): near = lax.ppermute(own, 'band', swap)]
    pallas_call x1, Pallas kernels: 6.78 us -> 17.5 us  [on_device(): pl.pallas_call(functools.partial(gram_kernel, pairs=pairs, bands=bands, g...]
  transfers between devices with their start and end apart: 20 -> 20, of which waited for: 8 -> 6; matrix products, arithmetic and copies ran while one was open for 2% -> 3% of each run, Pallas kernels for 22% -> 34%
where the time goes in v2:
time: 141 us
  Pallas kernels  73.6 us (52%)
  starting transfers between devices  29.7 us (21%)
  waiting for transfers between devices  28.9 us (20%)
  local copies, waits for them, and re-layouts  8.24 us (6%)
    pallas_call x4, Pallas kernels, on_device(): pieces = forecast(info, own, near, far, w1, b1, w2, b2)  47.5 us
    ppermute x4, waiting for transfers between devices, on_device(): near = lax.ppermute(own, 'band', swap)  18.4 us
    pallas_call x1, Pallas kernels, on_device(): pl.pallas_call(functools.partial(gram_kernel, pairs=pairs, bands=bands, g...  17.5 us
    ppermute x4, starting transfers between devices, on_device(): far = lax.ppermute(near, 'band', forward)  16.3 us
    ppermute x12, waiting for transfers between devices, on_device(): piece = lax.ppermute(piece, 'grp', [(i, i ^ step) for i in range(groups)])  10.5 us
    pallas_call x1, Pallas kernels, on_device(): pl.pallas_call(functools.partial(analysis_kernel, members=members, chans=...  8.5 us
    ppermute x12, starting transfers between devices, on_device(): piece = lax.ppermute(piece, 'grp', [(i, i ^ step) for i in range(groups)])  8.15 us
    ppermute x4, starting transfers between devices, on_device(): near = lax.ppermute(own, 'band', swap)  5.23 us
  transfers between devices with their start and end apart: 20, of which 6 were waited for; matrix products, arithmetic and copies ran while one was open for 3% of the time, Pallas kernels for 34%

profile of v2, /device:TPU:0, one launch (start us, length us, event | category | flops | bytes accessed | tf_op | source)
XLA Modules:
  0.0 141.0 jit_solution(7347422539817875340)
XLA Ops:
  0.0 2.8 %fusion.4 = (bf16[2,69,2,1024]{3,2,1,0:T(2,128)(2,1)S(1)}, bf16[2,69,2,1024]{3,2,1,0:T(2,128)(2,1)S(1)}, bf16[2,69,2,1024]{3,2,1,0:T(2,128)(2,1)S(1)}, bf16[2,69,2,1024]{3,2,1,0:T(2,128)(2,1)S(1)}) fusion(bf16[8,69,2,1024]{3,2,1,0:T(2,128)(2,1)} %param.10), kind=kLoop, calls=%fused_computation.18 | loop fusion | bytes 4521984 | tf_op jit(solution)/shard_map/slice | solution.py:299
  3.0 3.0 %collective-permute-start = (bf16[2,2,72,1024]{3,2,1,0:T(8,128)(2,1)S(1)}, bf16[2,2,72,1024]{3,2,1,0:T(8,128)(2,1)}, u32[]{:S(2)}, u32[]{:S(2)}) collective-permute-start(bf16[2,2,72,1024]{3,2,1,0:T(8,128)(2,1)S(1)} %pad.29.own), channel_id=1, source_target_pairs={{0,1},{1,0},{2,3},{3,2},{4,5},{5,4},{6,7},{7,6},{8,9},{9,8},{10,11... | collective-permute-start | bytes 1769480 | tf_op jit(solution)/shard_map/ppermute | solution.py:301
  6.3 14.0 %collective-permute-done.near = bf16[2,2,72,1024]{3,2,1,0:T(8,128)(2,1)} collective-permute-done((bf16[2,2,72,1024]{3,2,1,0:T(8,128)(2,1)S(1)}, bf16[2,2,72,1024]{3,2,1,0:T(8,128)(2,1)}, u32[]{:S(2)}, u32[]{:S(2)}) %collective-permute-start) | collective-permute-done | bytes 589856 | tf_op jit(solution)/shard_map/ppermute | solution.py:301
  20.3 4.9 %collective-permute-start.1 = (bf16[2,2,72,1024]{3,2,1,0:T(8,128)(2,1)}, bf16[2,2,72,1024]{3,2,1,0:T(8,128)(2,1)}, u32[]{:S(2)}, u32[]{:S(2)}) collective-permute-start(bf16[2,2,72,1024]{3,2,1,0:T(8,128)(2,1)} %collective-permute-done.near), channel_id=1, source_target_pairs={{3,1},{5,3},{7,5},{0,2},{2,4},{4,6},{11,9},{13,11},{15,13},{8,10},... | collective-permute-start | bytes 1769480 | tf_op jit(solution)/shard_map/ppermute | solution.py:304
  25.7 2.1 %collective-permute-start.15 = (bf16[2,2,72,1024]{3,2,1,0:T(8,128)(2,1)S(1)}, bf16[2,2,72,1024]{3,2,1,0:T(8,128)(2,1)}, u32[]{:S(2)}, u32[]{:S(2)}) collective-permute-start(bf16[2,2,72,1024]{3,2,1,0:T(8,128)(2,1)S(1)} %pad.36.own), channel_id=1, source_target_pairs={{0,1},{1,0},{2,3},{3,2},{4,5},{5,4},{6,7},{7,6},{8,9},{9,8},{10,11... | collective-permute-start | bytes 1769480 | tf_op jit(solution)/shard_map/ppermute | solution.py:301
  27.8 0.8 pad_bitcast_fusion
  28.5 4.4 %collective-permute-done.5.near = bf16[2,2,72,1024]{3,2,1,0:T(8,128)(2,1)} collective-permute-done((bf16[2,2,72,1024]{3,2,1,0:T(8,128)(2,1)S(1)}, bf16[2,2,72,1024]{3,2,1,0:T(8,128)(2,1)}, u32[]{:S(2)}, u32[]{:S(2)}) %collective-permute-start.5) | collective-permute-done | bytes 589856 | tf_op jit(solution)/shard_map/ppermute | solution.py:301
  32.9 4.9 %collective-permute-start.6 = (bf16[2,2,72,1024]{3,2,1,0:T(8,128)(2,1)}, bf16[2,2,72,1024]{3,2,1,0:T(8,128)(2,1)}, u32[]{:S(2)}, u32[]{:S(2)}) collective-permute-start(bf16[2,2,72,1024]{3,2,1,0:T(8,128)(2,1)} %collective-permute-done.5.near), channel_id=1, source_target_pairs={{3,1},{5,3},{7,5},{0,2},{2,4},{4,6},{11,9},{13,11},{15,13},{8,10},... | collective-permute-start | bytes 1769480 | tf_op jit(solution)/shard_map/ppermute | solution.py:304
  38.1 0.8 copy.46
  39.1 1.1 copy.30
  40.4 11.7 %forecast.4 = (bf16[2,144,256]{2,1,0:T(8,128)(2,1)S(1)}, bf16[2,144,256]{2,1,0:T(8,128)(2,1)S(1)}, bf16[2,144,256]{2,1,0:T(8,128)(2,1)S(1)}, bf16[2,144,256]{2,1,0:T(8,128)(2,1)S(1)}) custom-call(s32[4]{0:T(128)S(1)} %pad_add_fusion.info, bf16[2,2,72,1024]{3,2,1,0:T(8,128)(2,1)S(1)} %pad.29.own, bf16[2,2,72,1024]{3,2,1,0:T(8,128)(2,1)} %collective-permute-done.near, ...), custom_call_target="tpu_custom_call" | custom-call | flops 4831838208 | bytes 4194304 | tf_op jit(solution)/shard_map/forecast/pallas_call | solution.py:305
  52.1 3.5 %collective-permute-start.11 = (bf16[2,2,72,1024]{3,2,1,0:T(8,128)(2,1)}, bf16[2,2,72,1024]{3,2,1,0:T(8,128)(2,1)}, u32[]{:S(2)}, u32[]{:S(2)}) collective-permute-start(bf16[2,2,72,1024]{3,2,1,0:T(8,128)(2,1)} %collective-permute-done.10.near), channel_id=1, source_target_pairs={{3,1},{5,3},{7,5},{0,2},{2,4},{4,6},{11,9},{13,11},{15,13},{8,10},... | collective-permute-start | bytes 1769480 | tf_op jit(solution)/shard_map/ppermute | solution.py:304
  55.7 12.4 %forecast.5 = (bf16[2,144,256]{2,1,0:T(8,128)(2,1)S(1)}, bf16[2,144,256]{2,1,0:T(8,128)(2,1)}, bf16[2,144,256]{2,1,0:T(8,128)(2,1)S(1)}, bf16[2,144,256]{2,1,0:T(8,128)(2,1)S(1)}) custom-call(s32[4]{0:T(128)S(1)} %pad_add_fusion.info, bf16[2,2,72,1024]{3,2,1,0:T(8,128)(2,1)S(1)} %pad.34.own, bf16[2,2,72,1024]{3,2,1,0:T(8,128)(2,1)} %collective-permute-done.5.near, ...), custom_call_target="tpu_custom_call" | custom-call | flops 4831838208 | bytes 4194304 | tf_op jit(solution)/shard_map/forecast/pallas_call | solution.py:305
  68.0 0.6 copy-done.5
  68.7 3.1 %collective-permute-start.16 = (bf16[2,2,72,1024]{3,2,1,0:T(8,128)(2,1)}, bf16[2,2,72,1024]{3,2,1,0:T(8,128)(2,1)S(1)}, u32[]{:S(2)}, u32[]{:S(2)}) collective-permute-start(bf16[2,2,72,1024]{3,2,1,0:T(8,128)(2,1)} %collective-permute-done.15.near), channel_id=1, source_target_pairs={{3,1},{5,3},{7,5},{0,2},{2,4},{4,6},{11,9},{13,11},{15,13},{8,10},... | collective-permute-start | bytes 1769480 | tf_op jit(solution)/shard_map/ppermute | solution.py:304
  71.8 0.8 copy.51
  72.6 1.5 %collective-permute-start.3 = (bf16[2,144,256]{2,1,0:T(8,128)(2,1)}, bf16[2,144,256]{2,1,0:T(8,128)(2,1)S(1)}, u32[]{:S(2)}, u32[]{:S(2)}) collective-permute-start(bf16[2,144,256]{2,1,0:T(8,128)(2,1)} %copy-done.7), channel_id=1, source_target_pairs={{0,16},{8,24},{16,0},{24,8},{1,17},{9,25},{17,1},{25,9},{2,18},{10... | collective-permute-start | bytes 442376 | tf_op jit(solution)/shard_map/ppermute | solution.py:309
  74.1 0.3 collective-permute-start.4
  74.4 0.3 collective-permute-start.7
  74.7 11.7 %forecast.6 = (bf16[2,144,256]{2,1,0:T(8,128)(2,1)S(1)}, bf16[2,144,256]{2,1,0:T(8,128)(2,1)S(1)}, bf16[2,144,256]{2,1,0:T(8,128)(2,1)S(1)}, bf16[2,144,256]{2,1,0:T(8,128)(2,1)S(1)}) custom-call(s32[4]{0:T(128)S(1)} %pad_add_fusion.info, bf16[2,2,72,1024]{3,2,1,0:T(8,128)(2,1)S(1)} %pad.35.own, bf16[2,2,72,1024]{3,2,1,0:T(8,128)(2,1)} %collective-permute-done.10.near, ...), custom_call_target="tpu_custom_call" | custom-call | flops 4831838208 | bytes 4194304 | tf_op jit(solution)/shard_map/forecast/pallas_call | solution.py:305
  86.4 1.6 %collective-permute-start.8 = (bf16[2,144,256]{2,1,0:T(8,128)(2,1)S(1)}, bf16[2,144,256]{2,1,0:T(8,128)(2,1)S(1)}, u32[]{:S(2)}, u32[]{:S(2)}) collective-permute-start(bf16[2,144,256]{2,1,0:T(8,128)(2,1)S(1)} %copy-done.6), channel_id=1, source_target_pairs={{0,16},{8,24},{16,0},{24,8},{1,17},{9,25},{17,1},{25,9},{2,18},{10... | collective-permute-start | bytes 442376 | tf_op jit(solution)/shard_map/ppermute | solution.py:309
  88.1 0.6 collective-permute-start.12
  88.7 11.8 %forecast.7 = (bf16[2,144,256]{2,1,0:T(8,128)(2,1)S(1)}, bf16[2,144,256]{2,1,0:T(8,128)(2,1)S(1)}, bf16[2,144,256]{2,1,0:T(8,128)(2,1)S(1)}, bf16[2,144,256]{2,1,0:T(8,128)(2,1)S(1)}) custom-call(s32[4]{0:T(128)S(1)} %pad_add_fusion.info, bf16[2,2,72,1024]{3,2,1,0:T(8,128)(2,1)S(1)} %pad.36.own, bf16[2,2,72,1024]{3,2,1,0:T(8,128)(2,1)} %collective-permute-done.15.near, ...), custom_call_target="tpu_custom_call" | custom-call | flops 4831838208 | bytes 4194304 | tf_op jit(solution)/shard_map/forecast/pallas_call | solution.py:305
  100.6 1.6 %collective-permute-start.13 = (bf16[2,144,256]{2,1,0:T(8,128)(2,1)S(1)}, bf16[2,144,256]{2,1,0:T(8,128)(2,1)S(1)}, u32[]{:S(2)}, u32[]{:S(2)}) collective-permute-start(bf16[2,144,256]{2,1,0:T(8,128)(2,1)S(1)} %get-tuple-element.37), channel_id=1, source_target_pairs={{0,16},{8,24},{16,0},{24,8},{1,17},{9,25},{17,1},{25,9},{2,18},{10... | collective-permute-start | bytes 442376 | tf_op jit(solution)/shard_map/ppermute | solution.py:309
  102.2 0.6 collective-permute-start.17
  102.8 1.5 %collective-permute-start.18 = (bf16[2,144,256]{2,1,0:T(8,128)(2,1)S(1)}, bf16[2,144,256]{2,1,0:T(8,128)(2,1)S(1)}, u32[]{:S(2)}, u32[]{:S(2)}) collective-permute-start(bf16[2,144,256]{2,1,0:T(8,128)(2,1)S(1)} %get-tuple-element.42), channel_id=1, source_target_pairs={{0,16},{8,24},{16,0},{24,8},{1,17},{9,25},{17,1},{25,9},{2,18},{10... | collective-permute-start | bytes 442376 | tf_op jit(solution)/shard_map/ppermute | solution.py:309
  104.5 2.9 %collective-permute-done.13.rest_10_ = bf16[2,144,256]{2,1,0:T(8,128)(2,1)S(1)} collective-permute-done((bf16[2,144,256]{2,1,0:T(8,128)(2,1)S(1)}, bf16[2,144,256]{2,1,0:T(8,128)(2,1)S(1)}, u32[]{:S(2)}, u32[]{:S(2)}) %collective-permute-start.13) | collective-permute-done | bytes 147488 | tf_op jit(solution)/shard_map/ppermute | solution.py:309
  107.3 2.2 %collective-permute-done.14.rest_11_ = bf16[2,144,256]{2,1,0:T(8,128)(2,1)S(1)} collective-permute-done((bf16[2,144,256]{2,1,0:T(8,128)(2,1)S(1)}, bf16[2,144,256]{2,1,0:T(8,128)(2,1)S(1)}, u32[]{:S(2)}, u32[]{:S(2)}) %collective-permute-start.14) | collective-permute-done | bytes 147488 | tf_op jit(solution)/shard_map/ppermute | solution.py:309
  109.5 4.1 %collective-permute-done.18.rest_14_ = bf16[2,144,256]{2,1,0:T(8,128)(2,1)S(1)} collective-permute-done((bf16[2,144,256]{2,1,0:T(8,128)(2,1)S(1)}, bf16[2,144,256]{2,1,0:T(8,128)(2,1)S(1)}, u32[]{:S(2)}, u32[]{:S(2)}) %collective-permute-start.18) | collective-permute-done | bytes 147488 | tf_op jit(solution)/shard_map/ppermute | solution.py:309
  113.6 1.3 collective-permute-done.19.rest_15_
  114.9 17.5 %grams.1 = (bf16[2,9,256,256]{3,2,1,0:T(8,128)(2,1)S(1)}, f32[32,128]{1,0:T(8,128)S(1)}, f32[4,8,32,128]{3,2,1,0:T(8,128)S(1)}) custom-call(bf16[2,144,256]{2,1,0:T(8,128)(2,1)S(1)} %get-tuple-element.26.rest_0_, bf16[2,144,256]{2,1,0:T(8,128)(2,1)S(1)} %collective-permute-done.2.rest_1_, bf16[2,144,256]{2,1,0:T(8,128)(2,1)S(1)} %collective-permute-done.3.rest_2_, ...), custom_call_target="tpu_custom_call" | custom-call | tf_op jit(solution)/shard_map/grams/pallas_call | solution.py:314
  132.5 8.5 %analyse.1 = f32[8832,128]{1,0:T(8,128)} custom-call(s32[2,8]{1,0:T(2,128)S(1)} %copy-done.2, f32[2,8]{1,0:T(2,128)S(1)} %copy-done.3, f32[32,128]{1,0:T(8,128)S(1)} %get-tuple-element.44.mine, f32[4,8,32,128]{3,2,1,0:T(8,128)S(1)} %get-tuple-element.45.gathered, bf16[2,9,256,256]{3,2,1,0:T(8,128)(2,1)S(1)} %get-tuple-element.46.field), custom_call_target="tpu_custom_call" | custom-call | tf_op jit(solution)/shard_map/analyse/pallas_call | solution.py:342
  (69 shorter events, 1.8 us)
Async XLA Ops:
  3.0 17.3 %collective-permute-start = (bf16[2,2,72,1024]{3,2,1,0:T(8,128)(2,1)S(1)}, bf16[2,2,72,1024]{3,2,1,0:T(8,128)(2,1)}, u32[]{:S(2)}, u32[]{:S(2)}) collective-permute-start(bf16[2,2,72,1024]{3,2,1,0:T(8,128)(2,1)S(1)} %pad.29.own), channel_id=1, source_target_pairs={{0,1},{1,0},{2,3},{3,2},{4,5},{5,4},{6,7},{7,6},{8,9},{9,8},{10,11... | collective-permute-start | bytes 1769480 | tf_op jit(solution)/shard_map/ppermute | solution.py:301
  6.2 21.5 %copy-start.11 = (bf16[3,3,69,256]{3,2,1,0:T(8,128)(2,1)S(1)}, bf16[3,3,69,256]{3,2,1,0:T(8,128)(2,1)}, u32[]{:S(2)}) copy-start(bf16[3,3,69,256]{3,2,1,0:T(8,128)(2,1)} %param.13) | copy-start | bytes 953860
  6.2 26.7 %collective-permute-start.5 = (bf16[2,2,72,1024]{3,2,1,0:T(8,128)(2,1)S(1)}, bf16[2,2,72,1024]{3,2,1,0:T(8,128)(2,1)}, u32[]{:S(2)}, u32[]{:S(2)}) collective-permute-start(bf16[2,2,72,1024]{3,2,1,0:T(8,128)(2,1)S(1)} %pad.34.own), channel_id=1, source_target_pairs={{0,1},{1,0},{2,3},{3,2},{4,5},{5,4},{6,7},{7,6},{8,9},{9,8},{10,11... | collective-permute-start | bytes 1769480 | tf_op jit(solution)/shard_map/ppermute | solution.py:301
  20.3 20.1 %collective-permute-start.1 = (bf16[2,2,72,1024]{3,2,1,0:T(8,128)(2,1)}, bf16[2,2,72,1024]{3,2,1,0:T(8,128)(2,1)}, u32[]{:S(2)}, u32[]{:S(2)}) collective-permute-start(bf16[2,2,72,1024]{3,2,1,0:T(8,128)(2,1)} %collective-permute-done.near), channel_id=1, source_target_pairs={{3,1},{5,3},{7,5},{0,2},{2,4},{4,6},{11,9},{13,11},{15,13},{8,10},... | collective-permute-start | bytes 1769480 | tf_op jit(solution)/shard_map/ppermute | solution.py:304
  25.3 12.7 %copy-start.13 = (s32[2,256]{1,0:T(2,128)S(1)}, s32[2,256]{1,0:T(2,128)}, u32[]{:S(2)}) copy-start(s32[2,256]{1,0:T(2,128)} %param.15) | copy-start | bytes 6148
  25.3 13.5 %copy-start.10 = (bf16[3,3,256,69]{2,3,1,0:T(8,128)(2,1)S(1)}, bf16[3,3,256,69]{2,3,1,0:T(8,128)(2,1)}, u32[]{:S(2)}) copy-start(bf16[3,3,256,69]{2,3,1,0:T(8,128)(2,1)} %param.11) | copy-start | bytes 953860
  25.4 26.7 %collective-permute-start.10 = (bf16[2,2,72,1024]{3,2,1,0:T(8,128)(2,1)S(1)}, bf16[2,2,72,1024]{3,2,1,0:T(8,128)(2,1)}, u32[]{:S(2)}, u32[]{:S(2)}) collective-permute-start(bf16[2,2,72,1024]{3,2,1,0:T(8,128)(2,1)S(1)} %pad.35.own), channel_id=1, source_target_pairs={{0,1},{1,0},{2,3},{3,2},{4,5},{5,4},{6,7},{7,6},{8,9},{9,8},{10,11... | collective-permute-start | bytes 1769480 | tf_op jit(solution)/shard_map/ppermute | solution.py:301
  25.7 43.0 %collective-permute-start.15 = (bf16[2,2,72,1024]{3,2,1,0:T(8,128)(2,1)S(1)}, bf16[2,2,72,1024]{3,2,1,0:T(8,128)(2,1)}, u32[]{:S(2)}, u32[]{:S(2)}) collective-permute-start(bf16[2,2,72,1024]{3,2,1,0:T(8,128)(2,1)S(1)} %pad.36.own), channel_id=1, source_target_pairs={{0,1},{1,0},{2,3},{3,2},{4,5},{5,4},{6,7},{7,6},{8,9},{9,8},{10,11... | collective-permute-start | bytes 1769480 | tf_op jit(solution)/shard_map/ppermute | solution.py:301
  32.9 22.7 %collective-permute-start.6 = (bf16[2,2,72,1024]{3,2,1,0:T(8,128)(2,1)}, bf16[2,2,72,1024]{3,2,1,0:T(8,128)(2,1)}, u32[]{:S(2)}, u32[]{:S(2)}) collective-permute-start(bf16[2,2,72,1024]{3,2,1,0:T(8,128)(2,1)} %collective-permute-done.5.near), channel_id=1, source_target_pairs={{3,1},{5,3},{7,5},{0,2},{2,4},{4,6},{11,9},{13,11},{15,13},{8,10},... | collective-permute-start | bytes 1769480 | tf_op jit(solution)/shard_map/ppermute | solution.py:304
  52.1 15.9 %copy-start.4 = (bf16[2,144,256]{2,1,0:T(8,128)(2,1)}, bf16[2,144,256]{2,1,0:T(8,128)(2,1)S(1)}, u32[]{:S(2)}) copy-start(bf16[2,144,256]{2,1,0:T(8,128)(2,1)S(1)} %get-tuple-element.29) | copy-start | bytes 442372
  52.1 15.9 %copy-start.7 = (bf16[2,144,256]{2,1,0:T(8,128)(2,1)}, bf16[2,144,256]{2,1,0:T(8,128)(2,1)S(1)}, u32[]{:S(2)}) copy-start(bf16[2,144,256]{2,1,0:T(8,128)(2,1)S(1)} %get-tuple-element.28) | copy-start | bytes 442372
  52.1 15.9 %copy-start.8 = (bf16[2,144,256]{2,1,0:T(8,128)(2,1)}, bf16[2,144,256]{2,1,0:T(8,128)(2,1)S(1)}, u32[]{:S(2)}) copy-start(bf16[2,144,256]{2,1,0:T(8,128)(2,1)S(1)} %get-tuple-element.27) | copy-start | bytes 442372
  52.1 22.3 %collective-permute-start.11 = (bf16[2,2,72,1024]{3,2,1,0:T(8,128)(2,1)}, bf16[2,2,72,1024]{3,2,1,0:T(8,128)(2,1)}, u32[]{:S(2)}, u32[]{:S(2)}) collective-permute-start(bf16[2,2,72,1024]{3,2,1,0:T(8,128)(2,1)} %collective-permute-done.10.near), channel_id=1, source_target_pairs={{3,1},{5,3},{7,5},{0,2},{2,4},{4,6},{11,9},{13,11},{15,13},{8,10},... | collective-permute-start | bytes 1769480 | tf_op jit(solution)/shard_map/ppermute | solution.py:304
  68.7 19.4 %collective-permute-start.16 = (bf16[2,2,72,1024]{3,2,1,0:T(8,128)(2,1)}, bf16[2,2,72,1024]{3,2,1,0:T(8,128)(2,1)S(1)}, u32[]{:S(2)}, u32[]{:S(2)}) collective-permute-start(bf16[2,2,72,1024]{3,2,1,0:T(8,128)(2,1)} %collective-permute-done.15.near), channel_id=1, source_target_pairs={{3,1},{5,3},{7,5},{0,2},{2,4},{4,6},{11,9},{13,11},{15,13},{8,10},... | collective-permute-start | bytes 1769480 | tf_op jit(solution)/shard_map/ppermute | solution.py:304
  72.6 13.9 %collective-permute-start.2 = (bf16[2,144,256]{2,1,0:T(8,128)(2,1)}, bf16[2,144,256]{2,1,0:T(8,128)(2,1)S(1)}, u32[]{:S(2)}, u32[]{:S(2)}) collective-permute-start(bf16[2,144,256]{2,1,0:T(8,128)(2,1)} %copy-done.8), channel_id=1, source_target_pairs={{0,8},{8,0},{16,24},{24,16},{1,9},{9,1},{17,25},{25,17},{2,10},{10... | collective-permute-start | bytes 442376 | tf_op jit(solution)/shard_map/ppermute | solution.py:309
  72.6 15.5 %collective-permute-start.3 = (bf16[2,144,256]{2,1,0:T(8,128)(2,1)}, bf16[2,144,256]{2,1,0:T(8,128)(2,1)S(1)}, u32[]{:S(2)}, u32[]{:S(2)}) collective-permute-start(bf16[2,144,256]{2,1,0:T(8,128)(2,1)} %copy-done.7), channel_id=1, source_target_pairs={{0,16},{8,24},{16,0},{24,8},{1,17},{9,25},{17,1},{25,9},{2,18},{10... | collective-permute-start | bytes 442376 | tf_op jit(solution)/shard_map/ppermute | solution.py:309
  74.1 26.5 %collective-permute-start.4 = (bf16[2,144,256]{2,1,0:T(8,128)(2,1)}, bf16[2,144,256]{2,1,0:T(8,128)(2,1)S(1)}, u32[]{:S(2)}, u32[]{:S(2)}) collective-permute-start(bf16[2,144,256]{2,1,0:T(8,128)(2,1)} %copy-done.4), channel_id=1, source_target_pairs={{0,24},{8,16},{16,8},{24,0},{1,25},{9,17},{17,9},{25,1},{2,26},{10... | collective-permute-start | bytes 442376 | tf_op jit(solution)/shard_map/ppermute | solution.py:309
  74.4 27.7 %collective-permute-start.7 = (bf16[2,144,256]{2,1,0:T(8,128)(2,1)}, bf16[2,144,256]{2,1,0:T(8,128)(2,1)S(1)}, u32[]{:S(2)}, u32[]{:S(2)}) collective-permute-start(bf16[2,144,256]{2,1,0:T(8,128)(2,1)} %get-tuple-element.31), channel_id=1, source_target_pairs={{0,8},{8,0},{16,24},{24,16},{1,9},{9,1},{17,25},{25,17},{2,10},{10... | collective-permute-start | bytes 442376 | tf_op jit(solution)/shard_map/ppermute | solution.py:309
  86.4 15.7 %collective-permute-start.8 = (bf16[2,144,256]{2,1,0:T(8,128)(2,1)S(1)}, bf16[2,144,256]{2,1,0:T(8,128)(2,1)S(1)}, u32[]{:S(2)}, u32[]{:S(2)}) collective-permute-start(bf16[2,144,256]{2,1,0:T(8,128)(2,1)S(1)} %copy-done.6), channel_id=1, source_target_pairs={{0,16},{8,24},{16,0},{24,8},{1,17},{9,25},{17,1},{25,9},{2,18},{10... | collective-permute-start | bytes 442376 | tf_op jit(solution)/shard_map/ppermute | solution.py:309
  88.0 14.7 %collective-permute-start.9 = (bf16[2,144,256]{2,1,0:T(8,128)(2,1)S(1)}, bf16[2,144,256]{2,1,0:T(8,128)(2,1)S(1)}, u32[]{:S(2)}, u32[]{:S(2)}) collective-permute-start(bf16[2,144,256]{2,1,0:T(8,128)(2,1)S(1)} %get-tuple-element.33), channel_id=1, source_target_pairs={{0,24},{8,16},{16,8},{24,0},{1,25},{9,17},{17,9},{25,1},{2,26},{10... | collective-permute-start | bytes 442376 | tf_op jit(solution)/shard_map/ppermute | solution.py:309
  88.1 16.2 %copy-start.9 = (s32[2,256]{0,1:T(8,128)S(1)}, s32[2,256]{0,1:T(8,128)}, u32[]{:S(2)}) copy-start(s32[2,256]{0,1:T(8,128)} %copy.46) | copy-start | bytes 6148
  88.1 16.2 %copy-start.12 = (pred[2,256]{0,1:T(8,128)(4,1)S(1)}, pred[2,256]{0,1:T(8,128)(4,1)}, u32[]{:S(2)}) copy-start(pred[2,256]{0,1:T(8,128)(4,1)} %copy.51) | copy-start | bytes 1540
  88.1 26.9 %copy-start = (f32[2,256]{1,0:T(2,128)S(1)}, f32[2,256]{1,0:T(2,128)}, u32[]{:S(2)}) copy-start(f32[2,256]{1,0:T(2,128)} %rest_18_.1) | copy-start | bytes 6148
  88.1 26.9 %copy-start.1 = (f32[2,256]{1,0:T(2,128)S(1)}, f32[2,256]{1,0:T(2,128)}, u32[]{:S(2)}) copy-start(f32[2,256]{1,0:T(2,128)} %rest_19_.1) | copy-start | bytes 6148
  88.1 16.2 %collective-permute-start.12 = (bf16[2,144,256]{2,1,0:T(8,128)(2,1)S(1)}, bf16[2,144,256]{2,1,0:T(8,128)(2,1)S(1)}, u32[]{:S(2)}, u32[]{:S(2)}) collective-permute-start(bf16[2,144,256]{2,1,0:T(8,128)(2,1)S(1)} %get-tuple-element.36), channel_id=1, source_target_pairs={{0,8},{8,0},{16,24},{24,16},{1,9},{9,1},{17,25},{25,17},{2,10},{10... | collective-permute-start | bytes 442376 | tf_op jit(solution)/shard_map/ppermute | solution.py:309
  100.5 32.0 %copy-start.2 = (s32[2,8]{1,0:T(2,128)S(1)}, s32[2,8]{1,0:T(2,128)}, u32[]{:S(2)}) copy-start(s32[2,8]{1,0:T(2,128)} %neighbours.1) | copy-start | bytes 196
  100.5 32.0 %copy-start.3 = (f32[2,8]{1,0:T(2,128)S(1)}, f32[2,8]{1,0:T(2,128)}, u32[]{:S(2)}) copy-start(f32[2,8]{1,0:T(2,128)} %weights.1) | copy-start | bytes 196
  100.6 6.8 %collective-permute-start.13 = (bf16[2,144,256]{2,1,0:T(8,128)(2,1)S(1)}, bf16[2,144,256]{2,1,0:T(8,128)(2,1)S(1)}, u32[]{:S(2)}, u32[]{:S(2)}) collective-permute-start(bf16[2,144,256]{2,1,0:T(8,128)(2,1)S(1)} %get-tuple-element.37), channel_id=1, source_target_pairs={{0,16},{8,24},{16,0},{24,8},{1,17},{9,25},{17,1},{25,9},{2,18},{10... | collective-permute-start | bytes 442376 | tf_op jit(solution)/shard_map/ppermute | solution.py:309
  102.2 7.4 %collective-permute-start.14 = (bf16[2,144,256]{2,1,0:T(8,128)(2,1)S(1)}, bf16[2,144,256]{2,1,0:T(8,128)(2,1)S(1)}, u32[]{:S(2)}, u32[]{:S(2)}) collective-permute-start(bf16[2,144,256]{2,1,0:T(8,128)(2,1)S(1)} %get-tuple-element.38), channel_id=1, source_target_pairs={{0,24},{8,16},{16,8},{24,0},{1,25},{9,17},{17,9},{25,1},{2,26},{10... | collective-permute-start | bytes 442376 | tf_op jit(solution)/shard_map/ppermute | solution.py:309
  102.2 7.4 %collective-permute-start.17 = (bf16[2,144,256]{2,1,0:T(8,128)(2,1)S(1)}, bf16[2,144,256]{2,1,0:T(8,128)(2,1)S(1)}, u32[]{:S(2)}, u32[]{:S(2)}) collective-permute-start(bf16[2,144,256]{2,1,0:T(8,128)(2,1)S(1)} %get-tuple-element.41), channel_id=1, source_target_pairs={{0,8},{8,0},{16,24},{24,16},{1,9},{9,1},{17,25},{25,17},{2,10},{10... | collective-permute-start | bytes 442376 | tf_op jit(solution)/shard_map/ppermute | solution.py:309
  102.8 10.9 %collective-permute-start.18 = (bf16[2,144,256]{2,1,0:T(8,128)(2,1)S(1)}, bf16[2,144,256]{2,1,0:T(8,128)(2,1)S(1)}, u32[]{:S(2)}, u32[]{:S(2)}) collective-permute-start(bf16[2,144,256]{2,1,0:T(8,128)(2,1)S(1)} %get-tuple-element.42), channel_id=1, source_target_pairs={{0,16},{8,24},{16,0},{24,8},{1,17},{9,25},{17,1},{25,9},{2,18},{10... | collective-permute-start | bytes 442376 | tf_op jit(solution)/shard_map/ppermute | solution.py:309
  104.3 10.6 %collective-permute-start.19 = (bf16[2,144,256]{2,1,0:T(8,128)(2,1)S(1)}, bf16[2,144,256]{2,1,0:T(8,128)(2,1)S(1)}, u32[]{:S(2)}, u32[]{:S(2)}) collective-permute-start(bf16[2,144,256]{2,1,0:T(8,128)(2,1)S(1)} %get-tuple-element.43), channel_id=1, source_target_pairs={{0,24},{8,16},{16,8},{24,0},{1,25},{9,17},{17,9},{25,1},{2,26},{10... | collective-permute-start | bytes 442376 | tf_op jit(solution)/shard_map/ppermute | solution.py:309
  (4 other events, 37.8 us)

commit v3 on v2

--- a/solution.py
+++ b/solution.py
@@ -9,6 +9,7 @@
 
 NS_ITERS = 6
 PAIR = 2
+AHEAD = 3
 ROWK = 224
 SMEM = pl.BlockSpec(memory_space=pltpu.SMEM)
 VMEM = pl.BlockSpec(memory_space=pltpu.VMEM)
@@ -16,15 +17,88 @@
 HIGH = lax.Precision.HIGHEST
 
 
-def forecast_kernel(info, own, near, far, w1, b1, w2, b2, *rest, chans, hid, lon, groups):
-    outs, (ext, hidden, fore) = rest[:groups], rest[groups:]
-    odd, grp = info[0], info[1]
+def forecast_kernel(
+    own, w1, b1, w2, b2, field, near, far, ext, hidden, fore, stage, swap_sems, pass_sems, part_sems,
+    *, chans, hid, lon, groups, bands
+):
+    grp, band = lax.axis_index("grp"), lax.axis_index("band")
+    odd = lax.rem(band, 2)
+    count = own.shape[0]
     width = lon // groups
-
-    for member in range(PAIR):
+    partner = band + 1 - 2 * odd
+    target = band + 2 - 4 * odd
+    origin = band - 2 + 4 * odd
+    sends = (target >= 0) & (target < bands)
+    receives = (origin >= 0) & (origin < bands)
+    barrier = pltpu.get_barrier_semaphore()
+
+    def greet(axis, peer):
+        pl.semaphore_signal(barrier, inc=1, device_id={axis: peer}, device_id_type=MESH)
+
+    greet("band", partner)
+    for step in range(1, groups):
+        greet("grp", jnp.bitwise_xor(grp, step))
+    pl.when(receives)(lambda: greet("band", origin))
+
+    @pl.when(jnp.logical_not(receives))
+    def _():
+        far[...] = jnp.zeros_like(far)
+
+    pl.semaphore_wait(barrier, groups + sends.astype(jnp.int32))
+
+    def swap(m):
+        return pltpu.make_async_remote_copy(
+            src_ref=own.at[m],
+            dst_ref=near.at[m],
+            send_sem=swap_sems.at[0, m],
+            recv_sem=swap_sems.at[1, m],
+            device_id={"band": partner},
+            device_id_type=MESH,
+        )
+
+    def onward(m):
+        return pltpu.make_async_remote_copy(
+            src_ref=near.at[m],
+            dst_ref=far.at[m],
+            send_sem=pass_sems.at[0, m],
+            recv_sem=pass_sems.at[1, m],
+            device_id={"band": target},
+            device_id_type=MESH,
+        )
+
+    def handout(pair, step):
+        rows = pl.ds(pl.multiple_of((grp * count + pair * PAIR) * 8, 16), 8 * PAIR)
+        return pltpu.make_async_remote_copy(
+            src_ref=stage.at[pair, step],
+            dst_ref=field.at[:, :, rows, :],
+            send_sem=part_sems.at[0, pair, step],
+            recv_sem=part_sems.at[1, pair, step],
+            device_id={"grp": jnp.bitwise_xor(grp, step)},
+            device_id_type=MESH,
+        )
+
+    for m in range(AHEAD):
+        swap(m).start()
+    swap(0).wait_recv()
+    pl.when(sends)(lambda: onward(0).start())
+
+    def one(pair, member):
+        m = pair * PAIR + member
+
+        @pl.when(m + 1 < count)
+        def _():
+            swap(m + 1).wait_recv()
+            pl.when(sends)(lambda: onward(m + 1).start())
+
+        @pl.when(m + AHEAD < count)
+        def _():
+            swap(m + AHEAD).start()
+
+        pl.when(receives)(lambda: onward(m).wait_recv())
+
         for source, base in ((own, 2), (near, 4 * (1 - odd)), (far, 4 * odd)):
             for row in range(2):
-                x = source[member, row].astype(jnp.float32)
+                x = source[m, row].astype(jnp.float32)
                 shifted = [
                     pltpu.roll(x, 1, 1),
                     x,
@@ -35,9 +109,9 @@
 
         for row in range(4):
             if row == 0:
-                keep = info[2]
+                keep = band > 0
             elif row == 3:
-                keep = info[3]
+                keep = band < bands - 1
             else:
                 keep = None
 
@@ -48,7 +122,7 @@
                 h = 0.5 * h
                 h = h + h * jnp.tanh(h)
                 if keep is not None:
-                    h = jnp.where(keep > 0, h, 0.0)
+                    h = jnp.where(keep, h, 0.0)
                 hidden[row * hid : (row + 1) * hid, cols] = h.astype(jnp.bfloat16)
                 return carry
 
@@ -64,7 +138,7 @@
                 pltpu.roll(summed[:chans], 1, 1)
                 + summed[chans : 2 * chans]
                 + pltpu.roll(summed[2 * chans :], lon - 1, 1)
-                + own[member, row].astype(jnp.float32)
+                + own[m, row].astype(jnp.float32)
                 + b2[...]
             )
             for part in range(groups):
@@ -73,10 +147,30 @@
                     chans // 8, 8, width
                 )
 
-    for step in range(groups):
+    def both(pair, carry):
+        for member in range(PAIR):
+            one(pair, member)
+        rows = pl.ds(pl.multiple_of((grp * count + pair * PAIR) * 8, 16), 8 * PAIR)
         for row in range(2):
-            block = fore[jnp.bitwise_xor(grp, step), row]
-            outs[step][row] = block.reshape(chans * PAIR, width).astype(jnp.bfloat16)
+            field[row, :, rows, :] = fore[grp, row].astype(jnp.bfloat16)
+            for step in range(1, groups):
+                stage[pair, step, row] = fore[jnp.bitwise_xor(grp, step), row].astype(jnp.bfloat16)
+        for step in range(1, groups):
+            handout(pair, step).start()
+        return carry
+
+    lax.fori_loop(0, count // PAIR, both, 0)
+
+    def finish(pair, carry):
+        for step in range(1, groups):
+            handout(pair, step).wait()
+        for member in range(PAIR):
+            m = pair * PAIR + member
+            swap(m).wait_send()
+            pl.when(sends)(lambda m=m: onward(m).wait_send())
+        return carry
+
+    lax.fori_loop(0, count // PAIR, finish, 0)
 
 
 def exchange_start(bands, groups):
@@ -125,12 +219,12 @@
         copy.wait()
 
 
-def gram_kernel(*rest, pairs, bands, groups, chans, members, nobs, width):
-    slabs = rest[: groups * pairs]
-    chan, col, obs, prec, field, packed, gathered, pred, band_sems, grp_sems = rest[groups * pairs :]
+def gram_kernel(
+    field, chan, col, obs, prec, packed, gathered, pred, band_sems, grp_sems,
+    *, bands, groups, chans, members, nobs, width
+):
     exchange_start(bands, groups)
     grp = lax.axis_index("grp")
-    blocks = chans // 8
     depth = chans * PAIR
     lane = lax.broadcasted_iota(jnp.int32, (nobs, depth), 1)
     lane_chan = (lane // 16) * 8 + lane % 8
@@ -145,22 +239,16 @@
             for v in range(PAIR)
         ]
         pick_col = col_iota == col[:, row : row + 1]
-        for step in range(groups):
-            source = jnp.bitwise_xor(grp, step)
-            for pair in range(pairs):
-                slab = slabs[pair * groups + step]
-                first = source * (pairs * PAIR) + pair * PAIR
-                values = slab[row]
-                for block in range(blocks):
-                    rows = pl.ds(pl.multiple_of(first * 8, 16), 16)
-                    field[row, block, rows, :] = values[block * 16 : (block + 1) * 16, :]
-                for v in range(PAIR):
-                    g = jnp.dot(selects[v], values, preferred_element_type=jnp.float32)
-                    g = jnp.where(pick_col, g, 0.0).astype(jnp.bfloat16)
-                    line = lax.dot_general(
-                        ones, g, (((1,), (1,)), ((), ())), preferred_element_type=jnp.float32
-                    )
-                    pred[first + v] = line
+
+        for first in range(0, members, PAIR):
+            values = field[row, :, first * 8 : (first + PAIR) * 8, :].reshape(depth, width)
+            for v in range(PAIR):
+                g = jnp.dot(selects[v], values, preferred_element_type=jnp.float32)
+                g = jnp.where(pick_col, g, 0.0).astype(jnp.bfloat16)
+                line = lax.dot_general(
+                    ones, g, (((1,), (1,)), ((), ())), preferred_element_type=jnp.float32
+                )
+                pred[first + v] = line
         predicted = pred[:, 0, :]
         mean = jnp.sum(predicted, axis=0, keepdims=True) * (1.0 / members)
         perturb = predicted - mean
@@ -262,9 +350,6 @@
     width = lon // groups
     nobs = obs_index.shape[1]
     chans = -(-real // 8) * 8
-    band = lax.axis_index("band")
-    grp = lax.axis_index("grp")
-    info = jnp.stack([band % 2, grp, band > 0, band < bands - 1]).astype(jnp.int32)
 
     w1 = jnp.pad(conv1_weight, ((0, 0), (0, 0), (0, 0), (0, chans - real)))
     w1 = jnp.transpose(w1, (2, 0, 1, 3)).reshape(hid, 3, 3 * chans)
@@ -274,47 +359,40 @@
     b1 = conv1_bias[:, None]
     b2 = jnp.pad(conv2_bias, (0, chans - real))[:, None]
 
-    swap = [(i, i ^ 1) for i in range(bands)]
-    forward = [(i, i - 2) for i in range(3, bands, 2)] + [(i, i + 2) for i in range(0, bands - 2, 2)]
     pairs = own_members // PAIR
-    depth = chans * PAIR
-    forecast = pl.pallas_call(
-        functools.partial(forecast_kernel, chans=chans, hid=hid, lon=lon, groups=groups),
-        out_shape=[jax.ShapeDtypeStruct((height, depth, width), jnp.bfloat16)] * groups,
-        in_specs=[SMEM] + [VMEM] * 7,
-        out_specs=[VMEM] * groups,
+    blocks = chans // 8
+    own = jnp.transpose(prior_samples, (0, 2, 1, 3))
+    own = jnp.pad(own, ((0, 0), (0, 0), (0, chans - real), (0, 0)))
+    halo = pltpu.VMEM((own_members, height, chans, lon), jnp.bfloat16)
+    field = pl.pallas_call(
+        functools.partial(
+            forecast_kernel, chans=chans, hid=hid, lon=lon, groups=groups, bands=bands
+        ),
+        out_shape=jax.ShapeDtypeStruct((height, blocks, members * 8, width), jnp.bfloat16),
+        in_specs=[VMEM] * 5,
+        out_specs=VMEM,
         scratch_shapes=[
+            halo,
+            halo,
             pltpu.VMEM((6, ROWK, lon), jnp.bfloat16),
             pltpu.VMEM((4 * hid, lon), jnp.bfloat16),
-            pltpu.VMEM((groups, height, chans // 8, 8 * PAIR, width), jnp.float32),
+            pltpu.VMEM((groups, height, blocks, 8 * PAIR, width), jnp.float32),
+            pltpu.VMEM((pairs, groups, height, blocks, 8 * PAIR, width), jnp.bfloat16),
+            pltpu.SemaphoreType.DMA((2, own_members)),
+            pltpu.SemaphoreType.DMA((2, own_members)),
+            pltpu.SemaphoreType.DMA((2, pairs, groups)),
         ],
-        compiler_params=pltpu.CompilerParams(vmem_limit_bytes=40 * 2**20),
-        cost_estimate=pl.CostEstimate(
-            flops=2 * PAIR * 6 * hid * 768 * lon, bytes_accessed=4 * 2**20, transcendentals=0
+        compiler_params=pltpu.CompilerParams(
+            vmem_limit_bytes=44 * 2**20, collective_id=2, has_side_effects=True
         ),
         name="forecast",
-    )
-    slabs = []
-    for pair in range(pairs):
-        own = prior_samples[pair * PAIR : (pair + 1) * PAIR]
-        own = jnp.pad(jnp.transpose(own, (0, 2, 1, 3)), ((0, 0), (0, 0), (0, chans - real), (0, 0)))
-        near = lax.ppermute(own, "band", swap)
-        if pair >= 2:
-            near, _ = lax.optimization_barrier((near, slabs[(pair - 2) * groups]))
-        far = lax.ppermute(near, "band", forward)
-        pieces = forecast(info, own, near, far, w1, b1, w2, b2)
-        for step in range(groups):
-            piece = pieces[step]
-            if step:
-                piece = lax.ppermute(piece, "grp", [(i, i ^ step) for i in range(groups)])
-            slabs.append(piece)
+    )(own, w1, b1, w2, b2)
 
     chan = (obs_index // width).T
     col = (obs_index % width).T
-    field, packed, gathered = pl.pallas_call(
+    packed, gathered = pl.pallas_call(
         functools.partial(
             gram_kernel,
-            pairs=pairs,
             bands=bands,
             groups=groups,
             chans=chans,
@@ -323,12 +401,11 @@
             width=width,
         ),
         out_shape=[
-            jax.ShapeDtypeStruct((height, chans // 8, members * 8, width), jnp.bfloat16),
             jax.ShapeDtypeStruct((members, 128), jnp.float32),
             jax.ShapeDtypeStruct((groups, bands, members, 128), jnp.float32),
         ],
-        in_specs=[VMEM] * (len(slabs) + 4),
-        out_specs=[VMEM] * 3,
+        in_specs=[VMEM] * 5,
+        out_specs=[VMEM] * 2,
         scratch_shapes=[
             pltpu.VMEM((members, 8, nobs), jnp.float32),
             pltpu.SemaphoreType.DMA((2, bands)),
@@ -338,7 +415,7 @@
             vmem_limit_bytes=40 * 2**20, collective_id=1, has_side_effects=True
         ),
         name="grams",
-    )(*slabs, chan, col, obs_values, obs_prec)
+    )(field, chan, col, obs_values, obs_prec)
     out = pl.pallas_call(
         functools.partial(analysis_kernel, members=members, chans=chans, real=real, width=width),
         out_shape=jax.ShapeDtypeStruct((members * real * 2 * height, 128), jnp.float32),

time: 141 us -> 111 us (0.79)
  starting transfers between devices: 29.7 us -> 0 us
  Pallas kernels: 73.6 us -> 103 us
  waiting for transfers between devices: 28.9 us -> 0 us
  local copies, waits for them, and re-layouts: 8.24 us -> 6.24 us
    ppermute x20 -> x0, starting transfers between devices: 29.7 us -> none  [the longest x4 16.3 us: on_device(): far = lax.ppermute(near, 'band', forward)]
    pallas_call x5 -> x2, Pallas kernels: 65.1 us -> 94.7 us  [the longest x1 73.9 us: on_device(): pl.pallas_call(functools.partial(forecast_kernel, chans=chans, hid=hid, l...]
    ppermute x20 -> x0, waiting for transfers between devices: 28.9 us -> none  [the longest x4 18.4 us: on_device(): near = lax.ppermute(own, 'band', swap)]
    slice x1 -> x0, local copies, waits for them, and re-layouts: 2.81 us -> none  [on_device(): own = prior_samples[pair * PAIR:(pair + 1) * PAIR]]
  transfers between devices with their start and end apart: 20 -> 0, of which waited for: 6 -> 0; matrix products, arithmetic and copies ran while one was open for 3% -> 0% of each run, Pallas kernels for 34% -> 0%
where the time goes in v3:
time: 111 us; the launch traced here: 110 us
  Pallas kernels  103 us (93%)
  local copies, waits for them, and re-layouts  6.24 us (6%)
    pallas_call x1, Pallas kernels, on_device(): pl.pallas_call(functools.partial(forecast_kernel, chans=chans, hid=hid, l...  73.9 us
    pallas_call x1, Pallas kernels, on_device(): pl.pallas_call(functools.partial(gram_kernel, bands=bands, groups=groups,...  20.8 us
    pallas_call x1, Pallas kernels, on_device(): pl.pallas_call(functools.partial(analysis_kernel, members=members, chans=...  8.49 us

profile of v3, /device:TPU:0, one launch (start us, length us, event | category | flops | bytes accessed | tf_op | source)
XLA Modules:
  0.0 110.4 jit_solution(13529794334778925847)
XLA Ops:
  0.0 0.7 pad_bitcast_fusion.1
  0.7 0.7 broadcast_compare_fusion
  1.3 0.2 copy.33
  1.5 0.1 copy.27.b2
  1.6 0.8 copy.26.b1
  2.4 0.8 copy.28
  3.3 0.0 copy-start.4
  3.3 0.1 fusion.1
  3.4 1.1 %pad.21 = bf16[3,3,256,72]{2,3,1,0:T(8,128)(2,1)S(1)} pad(bf16[3,3,256,69]{2,3,1,0:T(8,128)(2,1)} %param.11, bf16[]{:T(256)} %constant.25.clone.1), padding=0_0x0_0x0_0x0_3 | pad | bytes 649730 | tf_op jit(solution)/shard_map/jit(_pad)/pad | solution.py:354
  4.6 0.2 copy.25.w1
  4.8 1.0 pad_bitcast_fusion
  5.8 0.2 copy.24
  5.9 0.1 copy.36
  6.0 0.0 copy-done.4
  6.0 0.7 copy.38
  6.7 0.4 pad.20.own
  7.1 0.0 copy-start
  7.1 0.0 copy-start.1
  7.1 73.9 %forecast.1.field = bf16[2,9,256,256]{3,2,1,0:T(8,128)(2,1)S(1)} custom-call(bf16[8,2,72,1024]{3,2,1,0:T(8,128)(2,1)S(1)} %pad.20.own, bf16[256,672]{1,0:T(8,128)(2,1)S(1)} %copy.25.w1, f32[256,1]{1,0:T(8,128)S(1)} %copy.26.b1, bf16[216,768]{1,0:T(8,128)(2,1)S(1)} %bitcast.24, f32[72,1]{1,0:T(8,128)S(1)} %copy.27.b2), custom_call_target="tpu_custom_call" | custom-call | tf_op jit(solution)/shard_map/forecast/pallas_call | solution.py:367
  81.0 0.0 copy-done
  81.0 0.0 copy-done.1
  81.0 0.0 copy-start.2
  81.1 0.0 copy-start.3
  81.1 20.8 %grams.1 = (f32[32,128]{1,0:T(8,128)S(1)}, f32[4,8,32,128]{3,2,1,0:T(8,128)S(1)}) custom-call(bf16[2,9,256,256]{3,2,1,0:T(8,128)(2,1)S(1)} %forecast.1.field, s32[256,2]{1,0:T(8,128)S(1)} %get-tuple-element.10.chan, s32[256,2]{1,0:T(8,128)S(1)} %get-tuple-element.9.col, f32[2,256]{1,0:T(2,128)S(1)} %copy-done, f32[2,256]{1,0:T(2,128)S(1)} %copy-done.1), custom_call_target="tpu_custom_call" | custom-call | tf_op jit(solution)/shard_map/grams/pallas_call | solution.py:393
  101.9 0.0 copy-done.2
  101.9 0.0 copy-done.3
  101.9 8.5 %analyse.1 = f32[8832,128]{1,0:T(8,128)} custom-call(s32[2,8]{1,0:T(2,128)S(1)} %copy-done.2, f32[2,8]{1,0:T(2,128)S(1)} %copy-done.3, f32[32,128]{1,0:T(8,128)S(1)} %get-tuple-element.7.mine, f32[4,8,32,128]{3,2,1,0:T(8,128)S(1)} %get-tuple-element.8.gathered, bf16[2,9,256,256]{3,2,1,0:T(8,128)(2,1)S(1)} %forecast.1.field), custom_call_target="tpu_custom_call" | custom-call | tf_op jit(solution)/shard_map/analyse/pallas_call | solution.py:419
  (1 shorter events, 0.0 us)
Async XLA Ops:
  3.3 2.7 %copy-start.4 = (bf16[8,69,2,1024]{3,2,1,0:T(2,128)(2,1)S(1)}, bf16[8,69,2,1024]{3,2,1,0:T(2,128)(2,1)}, u32[]{:S(2)}) copy-start(bf16[8,69,2,1024]{3,2,1,0:T(2,128)(2,1)} %param.10) | copy-start | bytes 6782980
  7.1 73.9 %copy-start = (f32[2,256]{1,0:T(2,128)S(1)}, f32[2,256]{1,0:T(2,128)}, u32[]{:S(2)}) copy-start(f32[2,256]{1,0:T(2,128)} %obs.1) | copy-start | bytes 6148
  7.1 73.9 %copy-start.1 = (f32[2,256]{1,0:T(2,128)S(1)}, f32[2,256]{1,0:T(2,128)}, u32[]{:S(2)}) copy-start(f32[2,256]{1,0:T(2,128)} %prec.1) | copy-start | bytes 6148
  81.0 20.9 %copy-start.2 = (s32[2,8]{1,0:T(2,128)S(1)}, s32[2,8]{1,0:T(2,128)}, u32[]{:S(2)}) copy-start(s32[2,8]{1,0:T(2,128)} %neighbours.1) | copy-start | bytes 196
  81.1 20.9 %copy-start.3 = (f32[2,8]{1,0:T(2,128)S(1)}, f32[2,8]{1,0:T(2,128)}, u32[]{:S(2)}) copy-start(f32[2,8]{1,0:T(2,128)} %weights.1) | copy-start | bytes 196

commit v4 on v3

--- a/solution.py
+++ b/solution.py
@@ -17,8 +17,12 @@
 HIGH = lax.Precision.HIGHEST
 
 
+def as_column(line):
+    return jnp.transpose(jnp.broadcast_to(line, (8, line.shape[1])), (1, 0))[:, :1]
+
+
 def forecast_kernel(
-    own, w1, b1, w2, b2, field, near, far, ext, hidden, fore, stage, swap_sems, pass_sems, part_sems,
+    own, w1, b1, w2, b2, field, near, far, ext, hidden, fore, stage, bias1, bias2, swap_sems, pass_sems, part_sems,
     *, chans, hid, lon, groups, bands
 ):
     grp, band = lax.axis_index("grp"), lax.axis_index("band")
@@ -31,6 +35,8 @@
     sends = (target >= 0) & (target < bands)
     receives = (origin >= 0) & (origin < bands)
     barrier = pltpu.get_barrier_semaphore()
+    bias1[...] = as_column(b1[...])
+    bias2[...] = as_column(b2[...])
 
     def greet(axis, peer):
         pl.semaphore_signal(barrier, inc=1, device_id={axis: peer}, device_id_type=MESH)
@@ -118,7 +124,7 @@
             def tile(n, carry, row=row, keep=keep):
                 cols = pl.ds(pl.multiple_of(n * 256, 256), 256)
                 window = ext[row : row + 3, :, cols].reshape(3 * ROWK, 256)
-                h = jnp.dot(w1[...], window, preferred_element_type=jnp.float32) + b1[...]
+                h = jnp.dot(w1[...], window, preferred_element_type=jnp.float32) + bias1[...]
                 h = 0.5 * h
                 h = h + h * jnp.tanh(h)
                 if keep is not None:
@@ -126,7 +132,7 @@
                 hidden[row * hid : (row + 1) * hid, cols] = h.astype(jnp.bfloat16)
                 return carry
 
-            lax.fori_loop(0, lon // 256, tile, 0, unroll=2)
+            lax.fori_loop(0, lon // 256, tile, 0, unroll=4)
 
         for row in range(2):
             summed = jnp.dot(
@@ -139,7 +145,7 @@
                 + summed[chans : 2 * chans]
                 + pltpu.roll(summed[2 * chans :], lon - 1, 1)
                 + own[m, row].astype(jnp.float32)
-                + b2[...]
+                + bias2[...]
             )
             for part in range(groups):
                 piece = out[:, part * width : (part + 1) * width]
@@ -220,7 +226,7 @@
 
 
 def gram_kernel(
-    field, chan, col, obs, prec, packed, gathered, pred, band_sems, grp_sems,
+    field, index, obs, prec, packed, gathered, pred, band_sems, grp_sems,
     *, bands, groups, chans, members, nobs, width
 ):
     exchange_start(bands, groups)
@@ -233,12 +239,13 @@
     ones = jnp.ones((8, width), jnp.bfloat16)
     packed[...] = jnp.zeros_like(packed)
     for row in range(2):
-        pick_chan = lane_chan == chan[:, row : row + 1]
+        place = as_column(index[row : row + 1, :].astype(jnp.float32)).astype(jnp.int32)
+        pick_chan = lane_chan == lax.div(place, width)
         selects = [
             jnp.where(pick_chan & (lane_member == v), 1.0, 0.0).astype(jnp.bfloat16)
             for v in range(PAIR)
         ]
-        pick_col = col_iota == col[:, row : row + 1]
+        pick_col = col_iota == lax.rem(place, width)
 
         for first in range(0, members, PAIR):
             values = field[row, :, first * 8 : (first + PAIR) * 8, :].reshape(depth, width)
@@ -356,8 +363,8 @@
     w1 = jnp.pad(w1, ((0, 0), (0, 0), (0, ROWK - 3 * chans))).reshape(hid, 3 * ROWK)
     w2 = jnp.pad(conv2_weight, ((0, 0), (0, 0), (0, chans - real), (0, 0)))
     w2 = jnp.transpose(w2, (1, 2, 0, 3)).reshape(3 * chans, 3 * hid)
-    b1 = conv1_bias[:, None]
-    b2 = jnp.pad(conv2_bias, (0, chans - real))[:, None]
+    b1 = conv1_bias[None, :]
+    b2 = jnp.pad(conv2_bias, (0, chans - real))[None, :]
 
     pairs = own_members // PAIR
     blocks = chans // 8
@@ -378,6 +385,8 @@
             pltpu.VMEM((4 * hid, lon), jnp.bfloat16),
             pltpu.VMEM((groups, height, blocks, 8 * PAIR, width), jnp.float32),
             pltpu.VMEM((pairs, groups, height, blocks, 8 * PAIR, width), jnp.bfloat16),
+            pltpu.VMEM((hid, 1), jnp.float32),
+            pltpu.VMEM((chans, 1), jnp.float32),
             pltpu.SemaphoreType.DMA((2, own_members)),
             pltpu.SemaphoreType.DMA((2, own_members)),
             pltpu.SemaphoreType.DMA((2, pairs, groups)),
@@ -388,8 +397,6 @@
         name="forecast",
     )(own, w1, b1, w2, b2)
 
-    chan = (obs_index // width).T
-    col = (obs_index % width).T
     packed, gathered = pl.pallas_call(
         functools.partial(
             gram_kernel,
@@ -404,7 +411,7 @@
             jax.ShapeDtypeStruct((members, 128), jnp.float32),
             jax.ShapeDtypeStruct((groups, bands, members, 128), jnp.float32),
         ],
-        in_specs=[VMEM] * 5,
+        in_specs=[VMEM] * 4,
         out_specs=[VMEM] * 2,
         scratch_shapes=[
             pltpu.VMEM((members, 8, nobs), jnp.float32),
@@ -415,7 +422,7 @@
             vmem_limit_bytes=40 * 2**20, collective_id=1, has_side_effects=True
         ),
         name="grams",
-    )(field, chan, col, obs_values, obs_prec)
+    )(field, obs_index, obs_values, obs_prec)
     out = pl.pallas_call(
         functools.partial(analysis_kernel, members=members, chans=chans, real=real, width=width),
         out_shape=jax.ShapeDtypeStruct((members * real * 2 * height, 128), jnp.float32),

time: 111 us -> 107 us (0.964)
  local copies, waits for them, and re-layouts: 6.24 us -> 4.64 us
    pallas_call x1, Pallas kernels: 73.9 us -> 70 us  [on_device(): pl.pallas_call(functools.partial(forecast_kernel, chans=chans, hid=hid, l...]
    pallas_call x1, Pallas kernels: 20.8 us -> 23.2 us  [on_device(): pl.pallas_call(functools.partial(gram_kernel, bands=bands, groups=groups,...]
where the time goes in v4:
time: 107 us; the launch traced here: 106 us
  Pallas kernels  102 us (95%)
  local copies, waits for them, and re-layouts  4.64 us (4%)
    pallas_call x1, Pallas kernels, on_device(): pl.pallas_call(functools.partial(forecast_kernel, chans=chans, hid=hid, l...  70 us
    pallas_call x1, Pallas kernels, on_device(): pl.pallas_call(functools.partial(gram_kernel, bands=bands, groups=groups,...  23.2 us
    pallas_call x1, Pallas kernels, on_device(): pl.pallas_call(functools.partial(analysis_kernel, members=members, chans=...  8.48 us

profile of v4, /device:TPU:0, one launch (start us, length us, event | category | flops | bytes accessed | tf_op | source)
XLA Modules:
  0.0 106.5 jit_solution(3966838610597128343)
XLA Ops:
  0.0 0.0 copy-start.6
  0.0 0.8 pad_bitcast_fusion.1.b2
  0.8 1.0 pad.21
  1.8 0.2 copy.17.w1
  2.0 1.0 pad_bitcast_fusion
  3.0 0.2 copy.16
  3.2 0.1 copy.19
  3.3 0.0 copy-done.6
  3.3 0.7 copy.21
  4.0 0.0 copy-start.5
  4.0 0.3 pad.20.own
  4.3 0.4 copy-done.5
  4.7 0.0 copy-start
  4.7 0.0 copy-start.1
  4.7 0.0 copy-start.2
  4.7 70.0 %forecast.1.field = bf16[2,9,256,256]{3,2,1,0:T(8,128)(2,1)S(1)} custom-call(bf16[8,2,72,1024]{3,2,1,0:T(8,128)(2,1)S(1)} %pad.20.own, bf16[256,672]{1,0:T(8,128)(2,1)S(1)} %copy.17.w1, f32[1,256]{1,0:T(1,128)S(1)} %bitcast.21, bf16[216,768]{1,0:T(8,128)(2,1)S(1)} %bitcast.20, f32[1,72]{1,0:T(1,128)S(1)} %pad_bitcast_fusion.1.b2), custom_call_target="tpu_custom_call" | custom-call | tf_op jit(solution)/shard_map/forecast/pallas_call | solution.py:374
  74.7 0.0 copy-done
  74.7 0.0 copy-done.1
  74.7 0.0 copy-done.2
  74.7 0.0 copy-start.3
  74.7 0.0 copy-start.4
  74.7 23.2 %grams.1 = (f32[32,128]{1,0:T(8,128)S(1)}, f32[4,8,32,128]{3,2,1,0:T(8,128)S(1)}) custom-call(bf16[2,9,256,256]{3,2,1,0:T(8,128)(2,1)S(1)} %forecast.1.field, s32[2,256]{1,0:T(2,128)S(1)} %copy-done, f32[2,256]{1,0:T(2,128)S(1)} %copy-done.1, f32[2,256]{1,0:T(2,128)S(1)} %copy-done.2), custom_call_target="tpu_custom_call" | custom-call | tf_op jit(solution)/shard_map/grams/pallas_call | solution.py:400
  98.0 0.0 copy-done.3
  98.0 0.0 copy-done.4
  98.0 8.5 %analyse.1 = f32[8832,128]{1,0:T(8,128)} custom-call(s32[2,8]{1,0:T(2,128)S(1)} %copy-done.3, f32[2,8]{1,0:T(2,128)S(1)} %copy-done.4, f32[32,128]{1,0:T(8,128)S(1)} %get-tuple-element.7.mine, f32[4,8,32,128]{3,2,1,0:T(8,128)S(1)} %get-tuple-element.8.gathered, bf16[2,9,256,256]{3,2,1,0:T(8,128)(2,1)S(1)} %forecast.1.field), custom_call_target="tpu_custom_call" | custom-call | tf_op jit(solution)/shard_map/analyse/pallas_call | solution.py:426
  (1 shorter events, 0.0 us)
Async XLA Ops:
  0.0 3.3 %copy-start.6 = (bf16[8,69,2,1024]{3,2,1,0:T(2,128)(2,1)S(1)}, bf16[8,69,2,1024]{3,2,1,0:T(2,128)(2,1)}, u32[]{:S(2)}) copy-start(bf16[8,69,2,1024]{3,2,1,0:T(2,128)(2,1)} %param.10) | copy-start | bytes 6782980
  4.0 0.7 copy-start.5
  4.7 70.0 %copy-start = (s32[2,256]{1,0:T(2,128)S(1)}, s32[2,256]{1,0:T(2,128)}, u32[]{:S(2)}) copy-start(s32[2,256]{1,0:T(2,128)} %index.1) | copy-start | bytes 6148
  4.7 70.0 %copy-start.1 = (f32[2,256]{1,0:T(2,128)S(1)}, f32[2,256]{1,0:T(2,128)}, u32[]{:S(2)}) copy-start(f32[2,256]{1,0:T(2,128)} %obs.1) | copy-start | bytes 6148
  4.7 70.0 %copy-start.2 = (f32[2,256]{1,0:T(2,128)S(1)}, f32[2,256]{1,0:T(2,128)}, u32[]{:S(2)}) copy-start(f32[2,256]{1,0:T(2,128)} %prec.1) | copy-start | bytes 6148
  74.7 23.2 %copy-start.3 = (s32[2,8]{1,0:T(2,128)S(1)}, s32[2,8]{1,0:T(2,128)}, u32[]{:S(2)}) copy-start(s32[2,8]{1,0:T(2,128)} %neighbours.1) | copy-start | bytes 196
  74.7 23.2 %copy-start.4 = (f32[2,8]{1,0:T(2,128)S(1)}, f32[2,8]{1,0:T(2,128)}, u32[]{:S(2)}) copy-start(f32[2,8]{1,0:T(2,128)} %weights.1) | copy-start | bytes 196

commit v5 on v4

--- a/solution.py
+++ b/solution.py
@@ -9,7 +9,7 @@
 
 NS_ITERS = 6
 PAIR = 2
-AHEAD = 3
+AHEAD = 8
 ROWK = 224
 SMEM = pl.BlockSpec(memory_space=pltpu.SMEM)
 VMEM = pl.BlockSpec(memory_space=pltpu.VMEM)
@@ -83,7 +83,7 @@
             device_id_type=MESH,
         )
 
-    for m in range(AHEAD):
+    for m in range(min(AHEAD, count)):
         swap(m).start()
     swap(0).wait_recv()
     pl.when(sends)(lambda: onward(0).start())

time: 107 us -> 107 us (level)
  no operation moved by 1% of the time
where the time goes in v5:
time: 107 us; the launch traced here: 106 us
  Pallas kernels  102 us (95%)
  local copies, waits for them, and re-layouts  4.64 us (4%)
    pallas_call x1, Pallas kernels, on_device(): pl.pallas_call(functools.partial(forecast_kernel, chans=chans, hid=hid, l...  70 us
    pallas_call x1, Pallas kernels, on_device(): pl.pallas_call(functools.partial(gram_kernel, bands=bands, groups=groups,...  23.2 us
    pallas_call x1, Pallas kernels, on_device(): pl.pallas_call(functools.partial(analysis_kernel, members=members, chans=...  8.48 us

profile of v5, /device:TPU:0, one launch (start us, length us, event | category | flops | bytes accessed | tf_op | source)
XLA Modules:
  0.0 106.5 jit_solution(16916193054859735559)
XLA Ops:
  0.0 0.0 copy-start.6
  0.0 0.8 pad_bitcast_fusion.1.b2
  0.8 1.0 pad.21
  1.8 0.2 copy.17.w1
  2.0 1.0 pad_bitcast_fusion
  3.0 0.2 copy.16
  3.2 0.1 copy.19
  3.3 0.0 copy-done.6
  3.3 0.7 copy.21
  4.0 0.0 copy-start.5
  4.0 0.3 pad.20.own
  4.3 0.4 copy-done.5
  4.7 0.0 copy-start
  4.7 0.0 copy-start.1
  4.7 0.0 copy-start.2
  4.7 70.0 %forecast.1.field = bf16[2,9,256,256]{3,2,1,0:T(8,128)(2,1)S(1)} custom-call(bf16[8,2,72,1024]{3,2,1,0:T(8,128)(2,1)S(1)} %pad.20.own, bf16[256,672]{1,0:T(8,128)(2,1)S(1)} %copy.17.w1, f32[1,256]{1,0:T(1,128)S(1)} %bitcast.21, bf16[216,768]{1,0:T(8,128)(2,1)S(1)} %bitcast.20, f32[1,72]{1,0:T(1,128)S(1)} %pad_bitcast_fusion.1.b2), custom_call_target="tpu_custom_call" | custom-call | tf_op jit(solution)/shard_map/forecast/pallas_call | solution.py:374
  74.7 0.0 copy-done
  74.7 0.0 copy-done.1
  74.7 0.0 copy-done.2
  74.7 0.0 copy-start.3
  74.7 0.0 copy-start.4
  74.7 23.2 %grams.1 = (f32[32,128]{1,0:T(8,128)S(1)}, f32[4,8,32,128]{3,2,1,0:T(8,128)S(1)}) custom-call(bf16[2,9,256,256]{3,2,1,0:T(8,128)(2,1)S(1)} %forecast.1.field, s32[2,256]{1,0:T(2,128)S(1)} %copy-done, f32[2,256]{1,0:T(2,128)S(1)} %copy-done.1, f32[2,256]{1,0:T(2,128)S(1)} %copy-done.2), custom_call_target="tpu_custom_call" | custom-call | tf_op jit(solution)/shard_map/grams/pallas_call | solution.py:400
  98.0 0.0 copy-done.3
  98.0 0.0 copy-done.4
  98.0 8.5 %analyse.1 = f32[8832,128]{1,0:T(8,128)} custom-call(s32[2,8]{1,0:T(2,128)S(1)} %copy-done.3, f32[2,8]{1,0:T(2,128)S(1)} %copy-done.4, f32[32,128]{1,0:T(8,128)S(1)} %get-tuple-element.7.mine, f32[4,8,32,128]{3,2,1,0:T(8,128)S(1)} %get-tuple-element.8.gathered, bf16[2,9,256,256]{3,2,1,0:T(8,128)(2,1)S(1)} %forecast.1.field), custom_call_target="tpu_custom_call" | custom-call | tf_op jit(solution)/shard_map/analyse/pallas_call | solution.py:426
  (1 shorter events, 0.0 us)
Async XLA Ops:
  0.0 3.3 %copy-start.6 = (bf16[8,69,2,1024]{3,2,1,0:T(2,128)(2,1)S(1)}, bf16[8,69,2,1024]{3,2,1,0:T(2,128)(2,1)}, u32[]{:S(2)}) copy-start(bf16[8,69,2,1024]{3,2,1,0:T(2,128)(2,1)} %param.10) | copy-start | bytes 6782980
  4.0 0.7 copy-start.5
  4.7 70.0 %copy-start = (s32[2,256]{1,0:T(2,128)S(1)}, s32[2,256]{1,0:T(2,128)}, u32[]{:S(2)}) copy-start(s32[2,256]{1,0:T(2,128)} %index.1) | copy-start | bytes 6148
  4.7 70.0 %copy-start.1 = (f32[2,256]{1,0:T(2,128)S(1)}, f32[2,256]{1,0:T(2,128)}, u32[]{:S(2)}) copy-start(f32[2,256]{1,0:T(2,128)} %obs.1) | copy-start | bytes 6148
  4.7 70.0 %copy-start.2 = (f32[2,256]{1,0:T(2,128)S(1)}, f32[2,256]{1,0:T(2,128)}, u32[]{:S(2)}) copy-start(f32[2,256]{1,0:T(2,128)} %prec.1) | copy-start | bytes 6148
  74.7 23.2 %copy-start.3 = (s32[2,8]{1,0:T(2,128)S(1)}, s32[2,8]{1,0:T(2,128)}, u32[]{:S(2)}) copy-start(s32[2,8]{1,0:T(2,128)} %neighbours.1) | copy-start | bytes 196
  74.7 23.2 %copy-start.4 = (f32[2,8]{1,0:T(2,128)S(1)}, f32[2,8]{1,0:T(2,128)}, u32[]{:S(2)}) copy-start(f32[2,8]{1,0:T(2,128)} %weights.1) | copy-start | bytes 196
